TPU v7x, 256 devices: a whole 4x4x8 slice. The times are simulated.
256 devices in a mesh: row: 32 (over y, z), col: 8 (over x, core).
Axes of the slice: x: 4, y: 4, z: 8, core: 2. Of those that a mesh axis runs over, the one named last changes fastest.
Arguments:
- lower: bfloat16 [8, 32, 512, 1, 8, 512], P(None, 'row', None, None, 'col'), may hold values from -0.125 to 0.125
- slab: float32 [8, 32, 512, 128], P(None, 'row'), may hold values from -6 to 6
- inverses: float32 [1, 8, 512, 512], P(None, 'col'), may hold values from -0.12374368670764582 to 2, as said below
Outputs:
- reduced: float32 [8, 32, 512, 128], P('col', 'row')
Inputs may be any that keep to these rules, and one draw needn't show every extreme that they name: `inverses`: each block is lower triangular with a positive diagonal.
All inputs are finite; a program needn't handle non-finite values.
Results may differ from a plain program's by a relative error of at most 0.0075.
Values may be sent and summed in bfloat16 or wider, within the bound.
A program may use at most 64 MiB of HBM per device.

v0:
```python
import jax
import jax.numpy as jnp
from jax import lax
from jax.sharding import PartitionSpec as P


def spread(shard, axis, root):
    mine = lax.axis_index(axis) == root
    return lax.psum(jnp.where(mine, shard, jnp.zeros_like(shard)), axis)


def body(lower, slab, inverses):
    row_blocks = lower.shape[0]
    block_size = lower.shape[2]
    col_steps = lower.shape[3]
    slab_width = slab.shape[3]
    n_row = lax.axis_size("row")
    n_col = lax.axis_size("col")
    my_row = lax.axis_index("row")
    my_col = lax.axis_index("col")
    panel_blocks = lower.reshape(row_blocks, block_size, col_steps, block_size)
    right_side = slab.reshape(row_blocks, block_size, slab_width)
    inverse_blocks = inverses.reshape(col_steps, block_size, block_size)
    step_count = col_steps * n_col

    def block_total(own_partial, own_right):
        return own_right - lax.psum(own_partial, "col")

    def solve_block(residue, owner_row, column_step):
        inverse_block = lax.dynamic_index_in_dim(inverse_blocks, column_step, 0, keepdims=False)
        x_now = jnp.dot(
            inverse_block,
            residue,
            precision=lax.Precision.HIGHEST,
            preferred_element_type=jnp.float32,
        )
        x_low = x_now.astype(jnp.bfloat16)
        x_low = spread(x_low, "row", owner_row)
        return (x_now, x_low)

    def record(solved, x_now, slot_index, owner_row, owner_col):
        previous = lax.dynamic_index_in_dim(solved, slot_index, 0, keepdims=True)
        is_owner = (my_row == owner_row) & (my_col == owner_col)
        updated = jnp.where(is_owner, x_now[None], previous)
        return lax.dynamic_update_index_in_dim(solved, updated, slot_index, 0)

    def apply_column(partial_value, x_low, column_step, active):

        def add_column(current):
            column_blocks = lax.dynamic_index_in_dim(panel_blocks, column_step, 2, keepdims=False)
            product = jnp.dot(
                column_blocks.reshape(row_blocks * block_size, block_size),
                x_low,
                preferred_element_type=jnp.float32,
            )
            return current + product.reshape(row_blocks, block_size, slab_width)

        return lax.cond(active, add_column, lambda current: current, partial_value)

    empty_sums = jnp.zeros((row_blocks, block_size, slab_width), jnp.float32)

    def step_whole(turn, state_now):
        partial_value, solved = state_now
        owner_row = turn % n_row
        slot_index = turn // n_row
        owner_col = turn % n_col
        column_step = turn // n_col
        own_right = lax.dynamic_index_in_dim(right_side, slot_index, 0, keepdims=False)
        own_partial = lax.dynamic_index_in_dim(partial_value, slot_index, 0, keepdims=False)
        residue = block_total(own_partial, own_right)
        x_now, x_low = solve_block(residue, owner_row, column_step)
        solved = record(solved, x_now, slot_index, owner_row, owner_col)
        partial_value = apply_column(partial_value, x_low, column_step, my_col == owner_col)
        return (partial_value, solved)

    partial_value, solved = lax.fori_loop(0, step_count, step_whole, (empty_sums, empty_sums))
    global_rows = jnp.arange(row_blocks) * n_row + my_row
    done_rows = (global_rows < step_count)[:, None, None]
    owner_cols = (global_rows % n_col)[:, None, None]
    scatter_terms = jnp.where(
        done_rows,
        jnp.where(owner_cols == my_col, solved, 0.0),
        jnp.where(my_col == 0, right_side, 0.0) - partial_value,
    )
    summed = lax.psum_scatter(scatter_terms, "col", scatter_dimension=0, tiled=True)
    return summed.reshape(row_blocks // n_col, 1, block_size, slab_width)


def solution(mesh):
    in_specs = (
        P(None, "row", None, None, "col", None),
        P(None, "row", None, None),
        P(None, "col", None, None),
    )
    out_specs = P("col", "row", None, None)
    return jax.shard_map(body, mesh=mesh, in_specs=in_specs, out_specs=out_specs, check_vma=False)
```

profile of v0, /device:TPU:21, one launch (start us, length us, event | category | flops | bytes accessed | tf_op | source)
XLA Modules:
  0.0 1744.6 jit_solution(17943854636326518422)
XLA Ops:
  7.5 1.5 broadcast_in_dim.38.clone.1
  9.1 1688.7 %while.21 = (s32[]{:T(128)}, f32[8,512,128]{2,1,0:T(8,128)S(1)}, f32[8,512,128]{2,1,0:T(8,128)}, s32[]{:T(128)}, f32[8,512,128]{2,1,0:T(8,128)}, /*index=5*/f32[...) while((s32[]{:T(128)}, f32[8,512,128]{2,1,0:T(8,128)S(1)}, ...), condition=%wide.region_5.6_spmd, body=%wide.region_0.5_spmd.sunk | while | flops 940441600 | bytes 16253497 | solution.py:76
  9.9 1.0 constant_dynamic-slice_fusion.2
  10.8 0.8 copy.14
  11.7 64.9 %all-reduce.3.cloned.1.call-done = f32[512,128]{1,0:T(8,128)} async-done(((f32[512,128]{1,0:T(8,128)}), f32[512,128]{1,0:T(8,128)}) %all-reduce.3.cloned.1.call-update) | async-done | bytes 262160 | tf_op jit(solution)/shard_map/while/body/eval_jaxpr/psum | solution.py:27
  76.6 2.9 fusion.15
  79.6 1.7 bitcast_select_fusion.2
  81.3 1.1 copy.15
  83.1 135.4 %all-reduce.5.cloned.1.call-done = bf16[512,128]{0,1:T(8,128)(2,1)} async-done(((bf16[512,128]{0,1:T(8,128)(2,1)}), bf16[512,128]{0,1:T(8,128)(2,1)}) %all-reduce.5.cloned.1.call-update) | async-done | bytes 131088 | tf_op jit(solution)/shard_map/while/body/eval_jaxpr/psum | solution.py:9
  219.3 1.0 constant_dynamic-slice_fusion.2
  220.3 0.8 copy.14
  221.1 66.7 %all-reduce.3.cloned.1.call-done = f32[512,128]{1,0:T(8,128)} async-done(((f32[512,128]{1,0:T(8,128)}), f32[512,128]{1,0:T(8,128)}) %all-reduce.3.cloned.1.call-update) | async-done | bytes 262160 | tf_op jit(solution)/shard_map/while/body/eval_jaxpr/psum | solution.py:27
  287.9 2.9 fusion.15
  290.8 1.7 bitcast_select_fusion.2
  292.5 1.1 copy.15
  293.6 0.7 constant_dynamic-update-slice_fusion.2
  294.3 135.2 %all-reduce.5.cloned.1.call-done = bf16[512,128]{0,1:T(8,128)(2,1)} async-done(((bf16[512,128]{0,1:T(8,128)(2,1)}), bf16[512,128]{0,1:T(8,128)(2,1)}) %all-reduce.5.cloned.1.call-update) | async-done | bytes 131088 | tf_op jit(solution)/shard_map/while/body/eval_jaxpr/psum | solution.py:9
  430.4 1.0 constant_dynamic-slice_fusion.2
  431.3 0.8 copy.14
  432.2 65.3 %all-reduce.3.cloned.1.call-done = f32[512,128]{1,0:T(8,128)} async-done(((f32[512,128]{1,0:T(8,128)}), f32[512,128]{1,0:T(8,128)}) %all-reduce.3.cloned.1.call-update) | async-done | bytes 262160 | tf_op jit(solution)/shard_map/while/body/eval_jaxpr/psum | solution.py:27
  497.5 2.9 fusion.15
  500.5 1.7 bitcast_select_fusion.2
  502.2 1.1 copy.15
  504.0 135.2 %all-reduce.5.cloned.1.call-done = bf16[512,128]{0,1:T(8,128)(2,1)} async-done(((bf16[512,128]{0,1:T(8,128)(2,1)}), bf16[512,128]{0,1:T(8,128)(2,1)}) %all-reduce.5.cloned.1.call-update) | async-done | bytes 131088 | tf_op jit(solution)/shard_map/while/body/eval_jaxpr/psum | solution.py:9
  640.0 1.0 constant_dynamic-slice_fusion.2
  641.0 0.8 copy.14
  641.8 67.7 %all-reduce.3.cloned.1.call-done = f32[512,128]{1,0:T(8,128)} async-done(((f32[512,128]{1,0:T(8,128)}), f32[512,128]{1,0:T(8,128)}) %all-reduce.3.cloned.1.call-update) | async-done | bytes 262160 | tf_op jit(solution)/shard_map/while/body/eval_jaxpr/psum | solution.py:27
  709.5 2.9 fusion.15
  712.5 1.7 bitcast_select_fusion.2
  714.2 1.1 copy.15
  716.0 135.4 %all-reduce.5.cloned.1.call-done = bf16[512,128]{0,1:T(8,128)(2,1)} async-done(((bf16[512,128]{0,1:T(8,128)(2,1)}), bf16[512,128]{0,1:T(8,128)(2,1)}) %all-reduce.5.cloned.1.call-update) | async-done | bytes 131088 | tf_op jit(solution)/shard_map/while/body/eval_jaxpr/psum | solution.py:9
  852.2 1.0 constant_dynamic-slice_fusion.2
  853.2 0.8 copy.14
  854.0 65.6 %all-reduce.3.cloned.1.call-done = f32[512,128]{1,0:T(8,128)} async-done(((f32[512,128]{1,0:T(8,128)}), f32[512,128]{1,0:T(8,128)}) %all-reduce.3.cloned.1.call-update) | async-done | bytes 262160 | tf_op jit(solution)/shard_map/while/body/eval_jaxpr/psum | solution.py:27
  919.6 2.9 fusion.15
  922.6 1.7 bitcast_select_fusion.2
  924.3 1.1 copy.15
  926.1 135.3 %all-reduce.5.cloned.1.call-done = bf16[512,128]{0,1:T(8,128)(2,1)} async-done(((bf16[512,128]{0,1:T(8,128)(2,1)}), bf16[512,128]{0,1:T(8,128)(2,1)}) %all-reduce.5.cloned.1.call-update) | async-done | bytes 131088 | tf_op jit(solution)/shard_map/while/body/eval_jaxpr/psum | solution.py:9
  1062.2 1.0 constant_dynamic-slice_fusion.2
  1063.2 0.8 copy.14
  1064.0 69.2 %all-reduce.3.cloned.1.call-done = f32[512,128]{1,0:T(8,128)} async-done(((f32[512,128]{1,0:T(8,128)}), f32[512,128]{1,0:T(8,128)}) %all-reduce.3.cloned.1.call-update) | async-done | bytes 262160 | tf_op jit(solution)/shard_map/while/body/eval_jaxpr/psum | solution.py:27
  1133.2 2.9 fusion.15
  1136.1 1.7 bitcast_select_fusion.2
  1137.8 1.1 copy.15
  1139.6 135.2 %all-reduce.5.cloned.1.call-done = bf16[512,128]{0,1:T(8,128)(2,1)} async-done(((bf16[512,128]{0,1:T(8,128)(2,1)}), bf16[512,128]{0,1:T(8,128)(2,1)}) %all-reduce.5.cloned.1.call-update) | async-done | bytes 131088 | tf_op jit(solution)/shard_map/while/body/eval_jaxpr/psum | solution.py:9
  1274.9 3.5 conditional.2
  1274.9 3.5 fusion.2
  1278.5 0.7 dynamic-slice_bitcast_fusion.2
  1279.3 1.0 constant_dynamic-slice_fusion.2
  1280.3 0.8 copy.14
  1281.1 62.0 %all-reduce.3.cloned.1.call-done = f32[512,128]{1,0:T(8,128)} async-done(((f32[512,128]{1,0:T(8,128)}), f32[512,128]{1,0:T(8,128)}) %all-reduce.3.cloned.1.call-update) | async-done | bytes 262160 | tf_op jit(solution)/shard_map/while/body/eval_jaxpr/psum | solution.py:27
  1343.1 2.9 fusion.15
  1346.1 1.7 bitcast_select_fusion.2
  1347.8 1.1 copy.15
  1349.6 135.2 %all-reduce.5.cloned.1.call-done = bf16[512,128]{0,1:T(8,128)(2,1)} async-done(((bf16[512,128]{0,1:T(8,128)(2,1)}), bf16[512,128]{0,1:T(8,128)(2,1)}) %all-reduce.5.cloned.1.call-update) | async-done | bytes 131088 | tf_op jit(solution)/shard_map/while/body/eval_jaxpr/psum | solution.py:9
  1485.7 1.0 constant_dynamic-slice_fusion.2
  1486.6 0.8 copy.14
  1487.5 68.6 %all-reduce.3.cloned.1.call-done = f32[512,128]{1,0:T(8,128)} async-done(((f32[512,128]{1,0:T(8,128)}), f32[512,128]{1,0:T(8,128)}) %all-reduce.3.cloned.1.call-update) | async-done | bytes 262160 | tf_op jit(solution)/shard_map/while/body/eval_jaxpr/psum | solution.py:27
  1556.1 2.9 fusion.15
  1559.0 1.7 bitcast_select_fusion.2
  1560.7 1.1 copy.15
  1562.5 135.2 %all-reduce.5.cloned.1.call-done = bf16[512,128]{0,1:T(8,128)(2,1)} async-done(((bf16[512,128]{0,1:T(8,128)(2,1)}), bf16[512,128]{0,1:T(8,128)(2,1)}) %all-reduce.5.cloned.1.call-update) | async-done | bytes 131088 | tf_op jit(solution)/shard_map/while/body/eval_jaxpr/psum | solution.py:9
  1697.8 3.9 subtract_select_fusion
  1701.7 35.8 %reduce-scatter.2.cloned.1.call-done = f32[1,512,128]{2,1,0:T(8,128)} async-done(((f32[8,512,128]{2,1,0:T(8,128)}), f32[1,512,128]{2,1,0:T(8,128)}) %reduce-scatter.2.cloned.1.call-update) | async-done | bytes 262160 | tf_op jit(solution)/shard_map/reduce_scatter | solution.py:85
  (59 shorter events, 10.9 us)
Async XLA Ops:
  7.4 1.7 copy-start
  9.1 67.5 %all-reduce.3.cloned.1.call-start = ((), (), s32[]{:S(2)}) async-start(), calls=%async_computation.2 | async-start | bytes 524288 | tf_op jit(solution)/shard_map/while/body/eval_jaxpr/psum | solution.py:27
  9.8 208.7 %all-reduce.5.cloned.1.call-start = ((), (), s32[]{:S(2)}) async-start(), calls=%async_computation.3 | async-start | bytes 262144 | tf_op jit(solution)/shard_map/while/body/eval_jaxpr/psum | solution.py:9
  218.5 69.4 %all-reduce.3.cloned.1.call-start = ((), (), s32[]{:S(2)}) async-start(), calls=%async_computation.2 | async-start | bytes 524288 | tf_op jit(solution)/shard_map/while/body/eval_jaxpr/psum | solution.py:27
  219.2 210.3 %all-reduce.5.cloned.1.call-start = ((), (), s32[]{:S(2)}) async-start(), calls=%async_computation.3 | async-start | bytes 262144 | tf_op jit(solution)/shard_map/while/body/eval_jaxpr/psum | solution.py:9
  429.6 67.9 %all-reduce.3.cloned.1.call-start = ((), (), s32[]{:S(2)}) async-start(), calls=%async_computation.2 | async-start | bytes 524288 | tf_op jit(solution)/shard_map/while/body/eval_jaxpr/psum | solution.py:27
  430.3 208.9 %all-reduce.5.cloned.1.call-start = ((), (), s32[]{:S(2)}) async-start(), calls=%async_computation.3 | async-start | bytes 262144 | tf_op jit(solution)/shard_map/while/body/eval_jaxpr/psum | solution.py:9
  639.2 70.3 %all-reduce.3.cloned.1.call-start = ((), (), s32[]{:S(2)}) async-start(), calls=%async_computation.2 | async-start | bytes 524288 | tf_op jit(solution)/shard_map/while/body/eval_jaxpr/psum | solution.py:27
  640.0 211.4 %all-reduce.5.cloned.1.call-start = ((), (), s32[]{:S(2)}) async-start(), calls=%async_computation.3 | async-start | bytes 262144 | tf_op jit(solution)/shard_map/while/body/eval_jaxpr/psum | solution.py:9
  851.4 68.2 %all-reduce.3.cloned.1.call-start = ((), (), s32[]{:S(2)}) async-start(), calls=%async_computation.2 | async-start | bytes 524288 | tf_op jit(solution)/shard_map/while/body/eval_jaxpr/psum | solution.py:27
  852.1 209.2 %all-reduce.5.cloned.1.call-start = ((), (), s32[]{:S(2)}) async-start(), calls=%async_computation.3 | async-start | bytes 262144 | tf_op jit(solution)/shard_map/while/body/eval_jaxpr/psum | solution.py:9
  1061.4 71.8 %all-reduce.3.cloned.1.call-start = ((), (), s32[]{:S(2)}) async-start(), calls=%async_computation.2 | async-start | bytes 524288 | tf_op jit(solution)/shard_map/while/body/eval_jaxpr/psum | solution.py:27
  1062.1 212.8 %all-reduce.5.cloned.1.call-start = ((), (), s32[]{:S(2)}) async-start(), calls=%async_computation.3 | async-start | bytes 262144 | tf_op jit(solution)/shard_map/while/body/eval_jaxpr/psum | solution.py:9
  1278.4 64.7 %all-reduce.3.cloned.1.call-start = ((), (), s32[]{:S(2)}) async-start(), calls=%async_computation.2 | async-start | bytes 524288 | tf_op jit(solution)/shard_map/while/body/eval_jaxpr/psum | solution.py:27
  1279.3 205.6 %all-reduce.5.cloned.1.call-start = ((), (), s32[]{:S(2)}) async-start(), calls=%async_computation.3 | async-start | bytes 262144 | tf_op jit(solution)/shard_map/while/body/eval_jaxpr/psum | solution.py:9
  1484.9 71.2 %all-reduce.3.cloned.1.call-start = ((), (), s32[]{:S(2)}) async-start(), calls=%async_computation.2 | async-start | bytes 524288 | tf_op jit(solution)/shard_map/while/body/eval_jaxpr/psum | solution.py:27
  1485.6 212.2 %all-reduce.5.cloned.1.call-start = ((), (), s32[]{:S(2)}) async-start(), calls=%async_computation.3 | async-start | bytes 262144 | tf_op jit(solution)/shard_map/while/body/eval_jaxpr/psum | solution.py:9
  1697.8 39.7 %reduce-scatter.2.cloned.1.call-start = ((), (), s32[]{:S(2)}) async-start(), calls=%async_computation.1 | async-start | bytes 2359296 | tf_op jit(solution)/shard_map/reduce_scatter | solution.py:85
Sparse Core Ops, SparseCore 0:
  12.2 64.3 all-reduce.2
  80.5 137.9 all-reduce.4
  221.6 66.1 all-reduce.2
  291.6 137.9 all-reduce.4
  432.4 65.0 all-reduce.2
  501.2 137.9 all-reduce.4
  642.4 67.1 all-reduce.2
  713.4 137.9 all-reduce.4
  854.5 65.0 all-reduce.2
  923.3 137.9 all-reduce.4
  1064.5 68.6 all-reduce.2
  1136.9 137.9 all-reduce.4
  1281.6 61.5 all-reduce.2
  1346.9 137.9 all-reduce.4
  1487.7 68.3 all-reduce.2
  1559.8 137.9 all-reduce.4
Sparse Core Ops, SparseCore 1:
  1701.8 35.6 reduce-scatter.1
where the time goes:
time: 1750 us; the launch traced here: 1740 us
  waiting for transfers between devices  1650 us (94%)
  local copies, waits for them, and re-layouts  36.3 us (2%)
  matrix products  27 us (2%)
  other arithmetic  17.5 us (1%)
    psum x8, waiting for transfers between devices, spread(): return lax.psum(jnp.where(mine, shard, jnp.zeros_like(shard)), axis)  1080 us
    psum x8, waiting for transfers between devices, block_total(): return own_right - lax.psum(own_partial, 'col')  530 us
    reduce_scatter x1, waiting for transfers between devices, body(): lax.psum_scatter(scatter_terms, 'col', scatter_dimension=0, tiled=True)  35.8 us
  transfers between devices with their start and end apart: 17, of which 17 were waited for; matrix products, arithmetic and copies ran while one was open for 2% of the time, Pallas kernels for 0%

commit v1 on v0

v1 whole, which is shorter than its diff:
```python
import jax
import jax.numpy as jnp
from jax import lax
from jax.experimental import pallas as pl
from jax.experimental.pallas import tpu as pltpu
from jax.sharding import PartitionSpec as P

MESH = pl.DeviceIdType.MESH
F32 = jnp.float32
BF16 = jnp.bfloat16

N_Z, N_Y, N_X = 8, 4, 4
SOLVE_0 = (0, 0)
SOLVE_1 = (1, 0)
SOLVE_23 = (2, 1)
SOLVE_47 = (6, 4)
INVERSE_SENDS = (
    ((1, 1), SOLVE_1, 0),
    ((10, 2), SOLVE_23, 0),
    ((26, 3), SOLVE_23, 1),
    ((6, 5), SOLVE_47, 1),
    ((14, 6), SOLVE_47, 2),
    ((30, 7), SOLVE_47, 3),
)
BLOCK_SENDS = (
    ((3, 1), SOLVE_23, 0),
    ((3, 2), SOLVE_23, 1),
    ((5, 4), SOLVE_47, 0),
    ((6, 5), SOLVE_47, 1),
    ((7, 4), SOLVE_47, 2),
    ((7, 5), SOLVE_47, 3),
    ((7, 6), SOLVE_47, 4),
)


def special_pairs():
    pairs = {(s, t) for s, t, _ in INVERSE_SENDS} | {(s, t) for s, t, _ in BLOCK_SENDS}
    pairs |= {(SOLVE_1, (z, 1)) for z in range(N_Z)}
    pairs |= {((3, 0), SOLVE_23)}
    pairs |= {(SOLVE_23, (2, c)) for c in (2, 3)}
    pairs |= {(SOLVE_23, (r, c)) for c in (2, 3) for r in range(4, 8)}
    pairs |= {((r, c), SOLVE_47) for c in (1, 3) for r in range(4, 8)}
    pairs |= {(SOLVE_47, (6, c)) for c in (5, 6, 7)}
    pairs |= {(SOLVE_47, (r, 0)) for r in range(4, 8)}
    return sorted({tuple(sorted(p)) for p in pairs})


def kernel(
    lower, slab, inverses, out,
    panel, inv, inv_parts, blocks, right, right_own, x_own, x_stage, x_full, x_in,
    acc_f, acc_b, stage_f, stage_b, pair_out, pair_in, sums, cross_in,
    load_sem, send_sem, x_sem, x_in_sem, inv_sem, block_sem, acc_f_sem, acc_b_sem, pair_sem, cross_sem,
):
    row = lax.axis_index("row")
    col = lax.axis_index("col")
    y, z = row // N_Z, row % N_Z
    x, core = col // 2, col % 2
    half = panel.shape[1] // 2
    quarter = half // 2
    width = x_own.shape[1]

    def here(device):
        return (row == device[0]) & (col == device[1])

    def plane_row(r0, r1):
        return (row >= r0) & (row < r1)

    root_z = jnp.where(col < 2, col, jnp.where(col < 4, 2, 6))
    sibling = (row, col + 1 - 2 * core)
    pending = []

    def remote(src, dst, s, recv, device):
        return pltpu.make_async_remote_copy(
            src_ref=src, dst_ref=dst, send_sem=send_sem.at[s], recv_sem=recv, device_id=device, device_id_type=MESH
        )

    def send(when, src, dst, s, recv, device):
        remote(src, dst, s, recv, device).start()
        pending.append((when, s, src.shape, src.dtype))

    def arrived(dst, recv):
        remote(dst, dst, 0, recv, sibling).wait_recv()

    load_first = pltpu.make_async_copy(lower.at[0], panel.at[0], load_sem.at[0])
    load_rest = pltpu.make_async_copy(lower.at[pl.ds(1, 7)], panel.at[pl.ds(1, 7)], load_sem.at[1])
    load_inv = pltpu.make_async_copy(inverses, inv, load_sem.at[2])
    load_right = pltpu.make_async_copy(slab.at[0], right, load_sem.at[3])
    load_own = pltpu.make_async_copy(slab.at[col], right_own, load_sem.at[4])
    load_inv.start()
    load_right.start()
    load_first.start()
    load_rest.start()
    load_own.start()

    def clear_slot(slot):
        inv_parts[slot] = jnp.zeros(inv_parts.shape[1:], BF16)

    @pl.when(here(SOLVE_1))
    def _():
        clear_slot(0)

    @pl.when(here(SOLVE_23))
    def _():
        clear_slot(0)
        clear_slot(1)

    @pl.when(here(SOLVE_47))
    def _():
        clear_slot(1)
        clear_slot(2)
        clear_slot(3)

    barrier = pltpu.get_barrier_semaphore()

    def greet(device):
        pl.semaphore_signal(barrier, inc=1, device_id=device, device_id_type=MESH)

    greet(sibling)
    for d in range(1, N_X):
        greet((row, (x + d) % N_X * 2 + core))
    count = jnp.int32(N_X)
    is_root = z == root_z

    @pl.when(is_root)
    def _():
        for d in range(1, N_Z):
            greet((y * N_Z + (z + d) % N_Z, col))

    @pl.when(jnp.logical_not(is_root))
    def _():
        greet((y * N_Z + root_z, col))

    count += jnp.where(is_root, N_Z - 1, 1)

    @pl.when(is_root & (y == 0))
    def _():
        for d in range(1, N_Y):
            greet((d * N_Z + z, col))

    @pl.when(is_root & (y != 0))
    def _():
        greet((z, col))

    count += jnp.where(is_root, jnp.where(y == 0, N_Y - 1, 1), 0)
    partners = {}
    for a, b in special_pairs():
        partners.setdefault(a, []).append(b)
        partners.setdefault(b, []).append(a)
    for device, others in partners.items():
        count += jnp.where(here(device), len(others), 0)

        @pl.when(here(device))
        def _(others=others):
            for other in others:
                greet(other)

    pl.semaphore_wait(barrier, count)

    def split_inverse(slot):
        value = inv[...]
        high = value.astype(BF16)
        inv_parts[slot, 0] = high
        inv_parts[slot, 1] = (value - high.astype(F32)).astype(BF16)

    for source, solver, slot in BLOCK_SENDS:

        @pl.when(here(source))
        def _(source=source, solver=solver, slot=slot):
            send(source, lower.at[0], blocks.at[slot], 0, block_sem.at[slot], solver)

    def part(slot, piece, b):
        return inv_parts.at[slot, piece, pl.ds(b * quarter, quarter), pl.ds(0, (b + 1) * quarter)]

    is_source = here(INVERSE_SENDS[0][0])
    for source, _, _ in INVERSE_SENDS[1:]:
        is_source |= here(source)

    @pl.when(is_source)
    def _():
        load_inv.wait()
        split_inverse(0)

    for source, solver, slot in INVERSE_SENDS:

        @pl.when(here(source))
        def _(source=source, solver=solver, slot=slot):
            for piece in range(2):
                for b in range(4):
                    s = 1 + piece * 4 + b
                    send(source, part(0, piece, b), part(slot, piece, b), s, inv_sem.at[slot, piece, b], solver)

    def inverse_arrived(slot):
        for piece in range(2):
            for b in range(4):
                arrived(part(slot, piece, b), inv_sem.at[slot, piece, b])

    def solve(slot, total):
        high = total.astype(BF16)
        low = (total - high.astype(F32)).astype(BF16)
        both = jnp.concatenate([high, low], axis=1)

        def times(rows, depth):
            a = inv_parts[slot, 0, rows, :depth]
            b = inv_parts[slot, 1, rows, :depth]
            return jnp.dot(a, both[:depth], preferred_element_type=F32) + jnp.dot(
                b, both[:depth], preferred_element_type=F32
            )

        whole = jnp.concatenate([times(slice(0, half), half), times(slice(half, 2 * half), 2 * half)], axis=0)
        return whole[:, :width] + whole[:, width:]

    def product(block, value):
        return jnp.dot(block, value, preferred_element_type=F32)

    @pl.when(here(SOLVE_0))
    def _():
        load_inv.wait()
        split_inverse(0)
        load_right.wait()
        value = solve(0, right[...])
        x_own[...] = value.astype(BF16)
        x_full[0] = value

    column_root = [SOLVE_0, (1, 1), (2, 2), (2, 3), SOLVE_47, (6, 5), (6, 6), (6, 7)]
    in_plane = [(1, 2, 3, 4, 5, 6, 7), (), (0, 1, 3), (0, 1, 3)] + [(2, 1, 3, 0, 4, 7, 5)] * 4

    def spread_from_root(c):
        when = column_root[c]
        root_row = column_root[c][0]
        for i, target in enumerate(in_plane[c][:1]):
            send(when, x_own, x_own, 9 + i, x_sem, (target, c))
        for d in (2, 1, 3):
            send(when, x_own, x_own, 15 + d, x_sem, (d * N_Z + root_row, c))
        for i, target in enumerate(in_plane[c]):
            if i > 0:
                send(when, x_own, x_own, 9 + i, x_sem, (target, c))

    @pl.when(here(SOLVE_0))
    def _():
        spread_from_root(0)

    @pl.when(here(SOLVE_1))
    def _():
        load_right.wait()
        load_first.wait()
        inverse_arrived(0)
        arrived(x_own, x_sem)
        value = solve(0, right[...] - product(panel[0], x_own[...]))
        x_stage[0] = value.astype(BF16)
        x_full[0] = value
        for i, target in enumerate((2, 3, 1, 4, 5, 6, 7, 0)):
            send(SOLVE_1, x_stage.at[0], x_own, 9 + i, x_sem, (target, 1))

    def rows_of(c, r0, r1):
        return plane_row(r0, r1) & (col == c)

    @pl.when(rows_of(0, 2, 8))
    def _():
        load_right.wait()
        load_first.wait()
        arrived(x_own, x_sem)
        stage_f[...] = right[...] - product(panel[0], x_own[...])

    @pl.when(here((3, 0)))
    def _():
        send((3, 0), stage_f, acc_f.at[1], 19, acc_f_sem.at[1], SOLVE_23)

    to_sibling = rows_of(0, 2, 8) & (row != 3)

    @pl.when(to_sibling)
    def _():
        send(to_sibling, stage_f, acc_f.at[0], 19, acc_f_sem.at[0], sibling)

    for r in range(4, 8):

        @pl.when(here((r, 1)))
        def _(r=r):
            load_right.wait()
            load_first.wait()
            arrived(x_own, x_sem)
            arrived(acc_f.at[0], acc_f_sem.at[0])
            stage_f[...] = acc_f[0] - product(panel[0], x_own[...])
            send((r, 1), stage_f, acc_f.at[r - 2], 19, acc_f_sem.at[r - 2], SOLVE_47)

    @pl.when(here(SOLVE_23))
    def _():
        when = SOLVE_23
        load_right.wait()
        load_first.wait()
        arrived(acc_f.at[0], acc_f_sem.at[0])
        arrived(x_own, x_sem)
        total = acc_f[0] - product(panel[0], x_own[...])
        inverse_arrived(0)
        value = solve(0, total)
        x_stage[0] = value.astype(BF16)
        x_full[0] = value
        for i, r in enumerate((4, 5, 7, 6)):
            send(when, x_stage.at[0], x_own, 20 + i, x_sem, (r, 2))
        arrived(blocks.at[0], block_sem.at[0])
        arrived(acc_f.at[1], acc_f_sem.at[1])
        stage_f[...] = acc_f[1] - product(blocks[0], x_own[...])
        arrived(blocks.at[1], block_sem.at[1])
        total = stage_f[...] - product(blocks[1], x_stage[0])
        inverse_arrived(1)
        value = solve(1, total)
        x_stage[1] = value.astype(BF16)
        x_full[1] = value
        for i, r in enumerate((4, 5, 7, 6)):
            send(when, x_stage.at[1], x_own, 24 + i, x_sem, (r, 3))
        send(when, x_stage.at[0], x_own, 28, x_sem, (2, 2))
        send(when, x_stage.at[1], x_own, 29, x_sem, (2, 3))
        send(when, x_full.at[0], x_in, 30, x_in_sem, (2, 0))
        send(when, x_full.at[1], x_in, 31, x_in_sem, (3, 0))

    low_rows = rows_of(2, 4, 8)

    @pl.when(low_rows)
    def _():
        load_first.wait()
        arrived(x_own, x_sem)
        stage_f[...] = product(panel[0], x_own[...])
        send(low_rows, stage_f, acc_f.at[0], 19, acc_f_sem.at[0], sibling)

    for r in range(4, 8):

        @pl.when(here((r, 3)))
        def _(r=r):
            load_first.wait()
            arrived(acc_f.at[0], acc_f_sem.at[0])
            arrived(x_own, x_sem)
            stage_b[...] = (acc_f[0] + product(panel[0], x_own[...])).astype(BF16)
            send((r, 3), stage_b, acc_b.at[r - 4], 19, acc_b_sem.at[r - 4], SOLVE_47)

    @pl.when(here(SOLVE_47))
    def _():
        when = SOLVE_47
        load_inv.wait()
        split_inverse(0)
        load_first.wait()
        load_right.wait()
        place = {(1, 0): blocks.at[0], (2, 0): panel.at[0], (2, 1): blocks.at[1]}
        place |= {(3, 0): blocks.at[2], (3, 1): blocks.at[3], (3, 2): blocks.at[4]}
        for slot in range(5):
            arrived(blocks.at[slot], block_sem.at[slot])
        for slot in range(1, 4):
            inverse_arrived(slot)
        for q in range(4):
            arrived(acc_f.at[q + 2], acc_f_sem.at[q + 2])
            for j in range(q - 1):
                acc_f[q + 2] -= product(place[q, j][...], x_stage[j])
            total = acc_f[q + 2]
            if q > 0:
                total -= product(place[q, q - 1][...], x_stage[q - 1])
            arrived(acc_b.at[q], acc_b_sem.at[q])
            total -= acc_b[q].astype(F32)
            value = solve(q, total)
            x_stage[q] = value.astype(BF16)
            x_full[q] = value
            if q == 0:
                x_own[...] = x_stage[0]
            else:
                send(when, x_stage.at[q], x_own, 20 + q, x_sem, (6, 4 + q))
        spread_from_root(4)
        for q in range(4):
            send(when, x_full.at[q], x_in, 24 + q, x_in_sem, (4 + q, 0))

    waited = rows_of(0, 0, 8) | (plane_row(4, 8) & (col < 4)) | here(SOLVE_23) | here(SOLVE_47)

    @pl.when(jnp.logical_not(waited))
    def _():
        arrived(x_own, x_sem)

    for c in (1, 2, 3, 5, 6, 7):

        @pl.when(here(column_root[c]))
        def _(c=c):
            spread_from_root(c)

    relay = is_root & (y != 0)
    peers = [(i, (y * N_Z + (z + d) % N_Z, col)) for i, d in enumerate((4, 3, 5, 2, 6, 1, 7))]

    @pl.when(relay)
    def _():
        for i, peer in peers:
            send(relay, x_own, x_own, 9 + i, x_sem, peer)

    always = row >= 0
    waited_first = (plane_row(2, 8) & (col < 4)) | here(SOLVE_1) | here(SOLVE_47)
    waited_first = waited_first & jnp.logical_not((col > 1) & (row < 4)) & jnp.logical_not(here((2, 1)))
    waited_first = waited_first & jnp.logical_not(here((3, 1))) | here(SOLVE_23)

    @pl.when(jnp.logical_not(waited_first))
    def _():
        load_first.wait()

    load_rest.wait()
    value = x_own[...]
    for i in range(4):
        pair_out[i] = product(panel[2 * i + 1 - core], value).astype(BF16)
    send(always, pair_out, pair_in, 32, pair_sem, sibling)
    for i in range(4):
        sums[i] = product(panel[2 * i + core], value).astype(BF16)
    arrived(pair_in, pair_sem)
    for i in range(4):
        sums[i] = (sums[i].astype(F32) + pair_in[i].astype(F32)).astype(BF16)
    for d in (2, 1, 3):
        owner = (x + d) % N_X
        send(always, sums.at[owner], cross_in.at[d - 1], 32 + d, cross_sem.at[d - 1], (row, owner * 2 + core))

    load_own.wait()
    total = right_own[...] - sums[x].astype(F32)
    for d in range(3):
        arrived(cross_in.at[d], cross_sem.at[d])
        total -= cross_in[d].astype(F32)
    out[...] = total

    solved = plane_row(0, 8) & (col == 0)

    @pl.when(solved & (row < 2))
    def _():
        out[...] = x_full[0]

    @pl.when(solved & (row >= 2))
    def _():
        arrived(x_in, x_in_sem)
        out[...] = x_in[...]

    @pl.when(jnp.logical_not(is_source | here(SOLVE_0) | here(SOLVE_47)))
    def _():
        load_inv.wait()

    read_right = plane_row(2, 8) & (col == 0) | plane_row(4, 8) & (col == 1)
    read_right = read_right | here(SOLVE_0) | here(SOLVE_1) | here(SOLVE_23) | here(SOLVE_47)

    @pl.when(jnp.logical_not(read_right))
    def _():
        load_right.wait()

    buffers = [x_own, stage_f, pair_out]

    def same_size(shape, dtype):
        for buffer in buffers:
            if buffer.shape == shape and buffer.dtype == dtype:
                return buffer
        if shape == panel.shape[1:]:
            return panel.at[0]
        return part(0, 0, shape[1] // quarter - 1)

    for when, s, shape, dtype in pending:

        @pl.when(when if not isinstance(when, tuple) else here(when))
        def _(s=s, shape=shape, dtype=dtype):
            ref = same_size(shape, dtype)
            remote(ref, ref, s, x_sem, sibling).wait_send()


def body(lower, slab, inverses):
    row_blocks, _, order, _, _, _ = lower.shape
    width = slab.shape[3]
    vmem = pltpu.VMEM
    dma = pltpu.SemaphoreType.DMA
    scratch = [
        vmem((row_blocks, order, order), BF16),
        vmem((order, order), F32),
        vmem((4, 2, order, order), BF16),
        vmem((5, order, order), BF16),
        vmem((order, width), F32),
        vmem((order, width), F32),
        vmem((order, width), BF16),
        vmem((4, order, width), BF16),
        vmem((4, order, width), F32),
        vmem((order, width), F32),
        vmem((6, order, width), F32),
        vmem((4, order, width), BF16),
        vmem((order, width), F32),
        vmem((order, width), BF16),
        vmem((4, order, width), BF16),
        vmem((4, order, width), BF16),
        vmem((4, order, width), BF16),
        vmem((3, order, width), BF16),
        dma((5,)),
        dma((36,)),
        dma,
        dma,
        dma((4, 2, 4)),
        dma((5,)),
        dma((6,)),
        dma((4,)),
        dma,
        dma((3,)),
    ]
    result = pl.pallas_call(
        kernel,
        name="window_solve",
        out_shape=jax.ShapeDtypeStruct((order, width), F32),
        in_specs=[pl.BlockSpec(memory_space=pl.ANY)] * 3,
        out_specs=pl.BlockSpec(memory_space=pltpu.VMEM),
        scratch_shapes=scratch,
        compiler_params=pltpu.CompilerParams(
            collective_id=0, has_side_effects=True, vmem_limit_bytes=40 << 20
        ),
    )(
        lower.reshape(row_blocks, order, order),
        slab.reshape(row_blocks, order, width),
        inverses.reshape(order, order),
    )
    return result.reshape(1, 1, order, width)


def solution(mesh):
    in_specs = (
        P(None, "row", None, None, "col", None),
        P(None, "row", None, None),
        P(None, "col", None, None),
    )
    out_specs = P("col", "row", None, None)
    return jax.shard_map(body, mesh=mesh, in_specs=in_specs, out_specs=out_specs, check_vma=False)
```

time: 1750 us -> 83.7 us (0.05)
  the two profiles are of different devices: /device:TPU:21 before, /device:TPU:13 now
where the time goes in v1:
time: 83.7 us; the launch traced here: 83.5 us
  Pallas kernels  77.8 us (93%)
  local copies, waits for them, and re-layouts  5.71 us (7%)
    pallas_call x1, Pallas kernels, body(): pl.pallas_call(kernel, name='window_solve', out_shape=jax.ShapeDtypeStruc...  77.8 us
    unnamed x7, local copies, waits for them, and re-layouts  5.71 us

profile of v1, /device:TPU:13, one launch (start us, length us, event | category | flops | bytes accessed | tf_op | source)
XLA Modules:
  0.0 83.5 jit_solution(12206850437571503799)
XLA Ops:
  0.0 0.0 copy-start
  0.0 2.2 %copy-done = bf16[8,1,512,1,1,512]{5,2,4,3,1,0:T(8,128)(2,1)S(1)} copy-done((bf16[8,1,512,1,1,512]{5,2,4,3,1,0:T(8,128)(2,1)S(1)}, bf16[8,1,512,1,1,512]{5,2,4,3,1,0:T(8,128)(2,1)}, u32[]{:S(2)}) %copy-start) | copy-done | bytes 4194328
  2.2 0.0 copy-start.1
  2.2 1.6 %copy-done.1 = f32[8,1,512,128]{3,2,1,0:T(8,128)S(1)} copy-done((f32[8,1,512,128]{3,2,1,0:T(8,128)S(1)}, f32[8,1,512,128]{3,2,1,0:T(8,128)}, u32[]{:S(2)}) %copy-start.1) | copy-done | bytes 2097176
  3.8 0.0 copy-start.2
  3.8 1.2 %copy-done.2 = f32[1,1,512,512]{3,2,1,0:T(8,128)S(1)} copy-done((f32[1,1,512,512]{3,2,1,0:T(8,128)S(1)}, f32[1,1,512,512]{3,2,1,0:T(8,128)}, u32[]{:S(2)}) %copy-start.2) | copy-done | bytes 1048600
  5.0 77.8 %window_solve.1 = f32[512,128]{1,0:T(8,128)S(1)} custom-call(bf16[8,512,512]{2,1,0:T(8,128)(2,1)S(1)} %bitcast.4, f32[8,512,128]{2,1,0:T(8,128)S(1)} %bitcast.5, f32[512,512]{1,0:T(8,128)S(1)} %bitcast.6), custom_call_target="tpu_custom_call" | custom-call | tf_op jit(solution)/shard_map/window_solve/pallas_call | solution.py:492
  82.8 0.7 copy.5
Async XLA Ops:
  0.0 2.2 %copy-start = (bf16[8,1,512,1,1,512]{5,2,4,3,1,0:T(8,128)(2,1)S(1)}, bf16[8,1,512,1,1,512]{5,2,4,3,1,0:T(8,128)(2,1)}, u32[]{:S(2)}) copy-start(bf16[8,1,512,1,1,512]{5,2,4,3,1,0:T(8,128)(2,1)} %param.3) | copy-start | bytes 12582916
  2.2 1.6 %copy-start.1 = (f32[8,1,512,128]{3,2,1,0:T(8,128)S(1)}, f32[8,1,512,128]{3,2,1,0:T(8,128)}, u32[]{:S(2)}) copy-start(f32[8,1,512,128]{3,2,1,0:T(8,128)} %param.4) | copy-start | bytes 6291460
  3.8 1.2 %copy-start.2 = (f32[1,1,512,512]{3,2,1,0:T(8,128)S(1)}, f32[1,1,512,512]{3,2,1,0:T(8,128)}, u32[]{:S(2)}) copy-start(f32[1,1,512,512]{3,2,1,0:T(8,128)} %param.5) | copy-start | bytes 3145732

commit v2 on v1

--- a/solution.py
+++ b/solution.py
@@ -37,10 +37,11 @@
     pairs = {(s, t) for s, t, _ in INVERSE_SENDS} | {(s, t) for s, t, _ in BLOCK_SENDS}
     pairs |= {(SOLVE_1, (z, 1)) for z in range(N_Z)}
     pairs |= {((3, 0), SOLVE_23)}
-    pairs |= {(SOLVE_23, (2, c)) for c in (2, 3)}
-    pairs |= {(SOLVE_23, (r, c)) for c in (2, 3) for r in range(4, 8)}
+    pairs |= {(SOLVE_23, (r, c)) for c in (2, 3) for r in (4, 5, 7)}
+    pairs |= {((7, c), (6, c)) for c in (2, 3)}
+    pairs |= {(SOLVE_23, (2, c)) for c in range(8) if c != 1}
+    pairs |= {(SOLVE_47, (6, c)) for c in range(8) if c != 4}
     pairs |= {((r, c), SOLVE_47) for c in (1, 3) for r in range(4, 8)}
-    pairs |= {(SOLVE_47, (6, c)) for c in (5, 6, 7)}
     pairs |= {(SOLVE_47, (r, 0)) for r in range(4, 8)}
     return sorted({tuple(sorted(p)) for p in pairs})
 
@@ -48,8 +49,8 @@
 def kernel(
     lower, slab, inverses, out,
     panel, inv, inv_parts, blocks, right, right_own, x_own, x_stage, x_full, x_in,
-    acc_f, acc_b, stage_f, stage_b, pair_out, pair_in, sums, cross_in,
-    load_sem, send_sem, x_sem, x_in_sem, inv_sem, block_sem, acc_f_sem, acc_b_sem, pair_sem, cross_sem,
+    acc_f, acc_b, stage_f, stage_b, relays, pair_out, pair_in, sums, cross_in,
+    load_sem, send_sem, x_sem, x_in_sem, relay_sem, inv_sem, block_sem, acc_f_sem, acc_b_sem, pair_sem, cross_sem,
 ):
     row = lax.axis_index("row")
     col = lax.axis_index("col")
@@ -65,7 +66,7 @@
     def plane_row(r0, r1):
         return (row >= r0) & (row < r1)
 
-    root_z = jnp.where(col < 2, col, jnp.where(col < 4, 2, 6))
+    root_z = col
     sibling = (row, col + 1 - 2 * core)
     pending = []
 
@@ -119,29 +120,58 @@
     for d in range(1, N_X):
         greet((row, (x + d) % N_X * 2 + core))
     count = jnp.int32(N_X)
-    is_root = z == root_z
+    is_root = (z == root_z) & (col < 2)
 
     @pl.when(is_root)
     def _():
         for d in range(1, N_Z):
             greet((y * N_Z + (z + d) % N_Z, col))
 
-    @pl.when(jnp.logical_not(is_root))
+    @pl.when((col < 2) & (z != root_z))
     def _():
         greet((y * N_Z + root_z, col))
 
-    count += jnp.where(is_root, N_Z - 1, 1)
-
-    @pl.when(is_root & (y == 0))
+    count += jnp.where(is_root, N_Z - 1, jnp.where(col < 2, 1, 0))
+    is_relay = (z == 2) | (z == 6)
+    relay_z = jnp.where(col < 4, 2, 6)
+
+    @pl.when(is_relay)
+    def _():
+        for k in range(2, 8):
+
+            @pl.when((core == k % 2) & (z == (2 if k < 4 else 6)))
+            def _(k=k):
+                for d in range(1, N_Z):
+                    greet((y * N_Z + (z + d) % N_Z, k))
+
+                @pl.when(col != k)
+                def _():
+                    greet((row, k))
+
+    count += jnp.where(z == 2, N_Z - 1 + jnp.where(x == 1, 0, 1), 0)
+    count += jnp.where(z == 6, 2 * (N_Z - 1) + jnp.where(x >= 2, 1, 2), 0)
+
+    @pl.when(col >= 2)
+    def _():
+        for q in range(N_X):
+
+            @pl.when((z != relay_z) | (q != x))
+            def _(q=q):
+                greet((y * N_Z + relay_z, 2 * q + core))
+
+    count += jnp.where(col >= 2, jnp.where(z == jnp.where(col < 4, 2, 6), N_X - 1, N_X), 0)
+    in_line = is_root | is_relay
+
+    @pl.when(in_line & (y == 0))
     def _():
         for d in range(1, N_Y):
             greet((d * N_Z + z, col))
 
-    @pl.when(is_root & (y != 0))
+    @pl.when(in_line & (y != 0))
     def _():
         greet((z, col))
 
-    count += jnp.where(is_root, jnp.where(y == 0, N_Y - 1, 1), 0)
+    count += jnp.where(in_line, jnp.where(y == 0, N_Y - 1, 1), 0)
     partners = {}
     for a, b in special_pairs():
         partners.setdefault(a, []).append(b)
@@ -221,8 +251,8 @@
         x_own[...] = value.astype(BF16)
         x_full[0] = value
 
-    column_root = [SOLVE_0, (1, 1), (2, 2), (2, 3), SOLVE_47, (6, 5), (6, 6), (6, 7)]
-    in_plane = [(1, 2, 3, 4, 5, 6, 7), (), (0, 1, 3), (0, 1, 3)] + [(2, 1, 3, 0, 4, 7, 5)] * 4
+    column_root = [SOLVE_0, (1, 1)]
+    in_plane = [(1, 2, 3, 4, 5, 6, 7), ()]
 
     def spread_from_root(c):
         when = column_root[c]
@@ -282,6 +312,58 @@
             stage_f[...] = acc_f[0] - product(panel[0], x_own[...])
             send((r, 1), stage_f, acc_f.at[r - 2], 19, acc_f_sem.at[r - 2], SOLVE_47)
 
+    def scatter(when, slot, k, s):
+        solver = SOLVE_23 if k < 4 else SOLVE_47
+        for q in range(N_X):
+            device = (solver[0], 2 * q + k % 2)
+            if device != solver:
+                rows = pl.ds(q * quarter, quarter)
+                send(when, x_stage.at[slot, rows], relays.at[max(k // 2 - 2, 0)], s + q, relay_sem.at[max(k // 2 - 2, 0)], device)
+
+    own_rows = pl.ds(pl.multiple_of(x * quarter, quarter), quarter)
+    other_planes = [(d * N_Z + z, col) for d in range(1, N_Y)]
+    other_z = [y * N_Z + (z + d) % N_Z for d in (4, 3, 5, 2, 6, 1, 7)]
+
+    def relay_quarter(k):
+        solver = SOLVE_23 if k < 4 else SOLVE_47
+        slot = max(k // 2 - 2, 0)
+        piece = relays.at[slot]
+        first = 40 + 12 * slot
+
+        place = lambda: (z == solver[0]) & (core == k % 2)
+
+        @pl.when(place())
+        def _():
+            @pl.when(here(solver))
+            def _():
+                q = solver[1] // 2
+                relays[slot] = x_stage[k - 2 if k < 4 else k - 4, q * quarter : (q + 1) * quarter]
+
+            @pl.when(jnp.logical_not(here(solver)))
+            def _():
+                arrived(piece, relay_sem.at[slot])
+
+            @pl.when(y == 0)
+            def _():
+                for i, device in enumerate(other_planes):
+                    send(lambda: place() & (y == 0), piece, piece, first + i, relay_sem.at[slot], device)
+
+            for i, target in enumerate(other_z):
+                direct = (lambda target=target: (y != 0) | (target < 4)) if k < 4 else (lambda: True)
+
+                @pl.when(direct())
+                def _(i=i, target=target, direct=direct):
+                    wanted = lambda: place() & direct()
+                    send(wanted, piece, x_own.at[own_rows], first + 3 + i, x_sem, (target, k))
+
+            @pl.when(col == k)
+            def _():
+                x_own[own_rows] = relays[slot]
+
+            @pl.when(col != k)
+            def _():
+                send(lambda: place() & (col != k), piece, x_own.at[own_rows], first + 10, x_sem, (row, k))
+
     @pl.when(here(SOLVE_23))
     def _():
         when = SOLVE_23
@@ -294,8 +376,9 @@
         value = solve(0, total)
         x_stage[0] = value.astype(BF16)
         x_full[0] = value
-        for i, r in enumerate((4, 5, 7, 6)):
+        for i, r in enumerate((4, 5, 7)):
             send(when, x_stage.at[0], x_own, 20 + i, x_sem, (r, 2))
+        scatter(when, 0, 2, 26)
         arrived(blocks.at[0], block_sem.at[0])
         arrived(acc_f.at[1], acc_f_sem.at[1])
         stage_f[...] = acc_f[1] - product(blocks[0], x_own[...])
@@ -305,19 +388,24 @@
         value = solve(1, total)
         x_stage[1] = value.astype(BF16)
         x_full[1] = value
-        for i, r in enumerate((4, 5, 7, 6)):
-            send(when, x_stage.at[1], x_own, 24 + i, x_sem, (r, 3))
-        send(when, x_stage.at[0], x_own, 28, x_sem, (2, 2))
-        send(when, x_stage.at[1], x_own, 29, x_sem, (2, 3))
-        send(when, x_full.at[0], x_in, 30, x_in_sem, (2, 0))
-        send(when, x_full.at[1], x_in, 31, x_in_sem, (3, 0))
+        for i, r in enumerate((4, 5, 7)):
+            send(when, x_stage.at[1], x_own, 23 + i, x_sem, (r, 3))
+        scatter(when, 1, 3, 29)
+        send(when, x_full.at[0], x_in, 36, x_in_sem, (2, 0))
+        send(when, x_full.at[1], x_in, 37, x_in_sem, (3, 0))
 
     low_rows = rows_of(2, 4, 8)
+
+    def pass_on(c):
+        @pl.when(row == 7)
+        def _():
+            send((7, c), x_own, x_own, 9, x_sem, (6, c))
 
     @pl.when(low_rows)
     def _():
         load_first.wait()
         arrived(x_own, x_sem)
+        pass_on(2)
         stage_f[...] = product(panel[0], x_own[...])
         send(low_rows, stage_f, acc_f.at[0], 19, acc_f_sem.at[0], sibling)
 
@@ -326,8 +414,10 @@
         @pl.when(here((r, 3)))
         def _(r=r):
             load_first.wait()
+            arrived(x_own, x_sem)
+            if r == 7:
+                pass_on(3)
             arrived(acc_f.at[0], acc_f_sem.at[0])
-            arrived(x_own, x_sem)
             stage_b[...] = (acc_f[0] + product(panel[0], x_own[...])).astype(BF16)
             send((r, 3), stage_b, acc_b.at[r - 4], 19, acc_b_sem.at[r - 4], SOLVE_47)
 
@@ -356,25 +446,32 @@
             value = solve(q, total)
             x_stage[q] = value.astype(BF16)
             x_full[q] = value
-            if q == 0:
-                x_own[...] = x_stage[0]
-            else:
-                send(when, x_stage.at[q], x_own, 20 + q, x_sem, (6, 4 + q))
-        spread_from_root(4)
+            scatter(when, q, 4 + q, 20 + 4 * q)
         for q in range(4):
-            send(when, x_full.at[q], x_in, 24 + q, x_in_sem, (4 + q, 0))
-
-    waited = rows_of(0, 0, 8) | (plane_row(4, 8) & (col < 4)) | here(SOLVE_23) | here(SOLVE_47)
-
-    @pl.when(jnp.logical_not(waited))
+            send(when, x_full.at[q], x_in, 36 + q, x_in_sem, (4 + q, 0))
+
+    for k in range(2, 8):
+        relay_quarter(k)
+
+    waited = rows_of(0, 0, 8) | (plane_row(4, 8) & (col < 4)) | here(SOLVE_23)
+
+    @pl.when(jnp.logical_not(waited) & (col < 2))
     def _():
         arrived(x_own, x_sem)
 
-    for c in (1, 2, 3, 5, 6, 7):
-
-        @pl.when(here(column_root[c]))
-        def _(c=c):
-            spread_from_root(c)
+    @pl.when(jnp.logical_not(waited) & (col >= 2))
+    def _():
+        @pl.when(z != relay_z)
+        def _():
+            arrived(x_own, x_sem)
+
+        @pl.when(z == relay_z)
+        def _():
+            arrived(x_own.at[pl.ds(0, 3 * quarter)], x_sem)
+
+    @pl.when(here(column_root[1]))
+    def _():
+        spread_from_root(1)
 
     relay = is_root & (y != 0)
     peers = [(i, (y * N_Z + (z + d) % N_Z, col)) for i, d in enumerate((4, 3, 5, 2, 6, 1, 7))]
@@ -397,7 +494,7 @@
     value = x_own[...]
     for i in range(4):
         pair_out[i] = product(panel[2 * i + 1 - core], value).astype(BF16)
-    send(always, pair_out, pair_in, 32, pair_sem, sibling)
+    send(always, pair_out, pair_in, 64, pair_sem, sibling)
     for i in range(4):
         sums[i] = product(panel[2 * i + core], value).astype(BF16)
     arrived(pair_in, pair_sem)
@@ -405,7 +502,7 @@
         sums[i] = (sums[i].astype(F32) + pair_in[i].astype(F32)).astype(BF16)
     for d in (2, 1, 3):
         owner = (x + d) % N_X
-        send(always, sums.at[owner], cross_in.at[d - 1], 32 + d, cross_sem.at[d - 1], (row, owner * 2 + core))
+        send(always, sums.at[owner], cross_in.at[d - 1], 64 + d, cross_sem.at[d - 1], (row, owner * 2 + core))
 
     load_own.wait()
     total = right_own[...] - sums[x].astype(F32)
@@ -436,7 +533,7 @@
     def _():
         load_right.wait()
 
-    buffers = [x_own, stage_f, pair_out]
+    buffers = [x_own, stage_f, pair_out, relays.at[0]]
 
     def same_size(shape, dtype):
         for buffer in buffers:
@@ -448,7 +545,7 @@
 
     for when, s, shape, dtype in pending:
 
-        @pl.when(when if not isinstance(when, tuple) else here(when))
+        @pl.when(here(when) if isinstance(when, tuple) else when() if callable(when) else when)
         def _(s=s, shape=shape, dtype=dtype):
             ref = same_size(shape, dtype)
             remote(ref, ref, s, x_sem, sibling).wait_send()
@@ -474,14 +571,16 @@
         vmem((4, order, width), BF16),
         vmem((order, width), F32),
         vmem((order, width), BF16),
+        vmem((2, order // 4, width), BF16),
         vmem((4, order, width), BF16),
         vmem((4, order, width), BF16),
         vmem((4, order, width), BF16),
         vmem((3, order, width), BF16),
         dma((5,)),
-        dma((36,)),
+        dma((72,)),
         dma,
         dma,
+        dma((2,)),
         dma((4, 2, 4)),
         dma((5,)),
         dma((6,)),
@@ -493,11 +592,11 @@
         kernel,
         name="window_solve",
         out_shape=jax.ShapeDtypeStruct((order, width), F32),
-        in_specs=[pl.BlockSpec(memory_space=pl.ANY)] * 3,
+        in_specs=[pl.BlockSpec(memory_space=pltpu.HBM)] * 3,
         out_specs=pl.BlockSpec(memory_space=pltpu.VMEM),
         scratch_shapes=scratch,
         compiler_params=pltpu.CompilerParams(
-            collective_id=0, has_side_effects=True, vmem_limit_bytes=40 << 20
+            collective_id=0, has_side_effects=True, vmem_limit_bytes=60 << 20
         ),
     )(
         lower.reshape(row_blocks, order, order),

time: 83.7 us -> 64.9 us (0.78)
  the two profiles are of different devices: /device:TPU:13 before, /device:TPU:21 now
where the time goes in v2:
time: 64.9 us; the launch traced here: 64.8 us
  Pallas kernels  63.2 us (97%)
  local copies, waits for them, and re-layouts  1.67 us (3%)
    pallas_call x1, Pallas kernels, body(): pl.pallas_call(kernel, name='window_solve', out_shape=jax.ShapeDtypeStruc...  63.2 us
    unnamed x1, local copies, waits for them, and re-layouts  1.67 us

profile of v2, /device:TPU:21, one launch (start us, length us, event | category | flops | bytes accessed | tf_op | source)
XLA Modules:
  0.0 64.8 jit_solution(3887873413422728853)
XLA Ops:
  0.0 63.2 %window_solve.1 = f32[512,128]{1,0:T(8,128)} custom-call(bf16[8,512,512]{2,1,0:T(8,128)(2,1)} %bitcast.4, f32[8,512,128]{2,1,0:T(8,128)} %bitcast.5, f32[512,512]{1,0:T(8,128)} %bitcast.6), custom_call_target="tpu_custom_call" | custom-call | tf_op jit(solution)/shard_map/window_solve/pallas_call | solution.py:591
  63.2 1.7 %copy.5 = f32[1,1,512,128]{3,2,1,0:T(8,128)} copy(f32[1,1,512,128]{3,2,1,0:T(8,128)} %bitcast.7) | data formatting | bytes 524288

commit v3 on v2

--- a/solution.py
+++ b/solution.py
@@ -15,12 +15,14 @@
 SOLVE_23 = (2, 1)
 SOLVE_47 = (6, 4)
 INVERSE_SENDS = (
-    ((1, 1), SOLVE_1, 0),
-    ((10, 2), SOLVE_23, 0),
-    ((26, 3), SOLVE_23, 1),
-    ((6, 5), SOLVE_47, 1),
-    ((14, 6), SOLVE_47, 2),
-    ((30, 7), SOLVE_47, 3),
+    ((1, 1), SOLVE_1, 0, (0, 1)),
+    ((9, 2), SOLVE_23, 0, (0,)),
+    ((25, 2), SOLVE_23, 0, (1,)),
+    ((12, 3), SOLVE_23, 1, (0,)),
+    ((28, 3), SOLVE_23, 1, (1,)),
+    ((6, 5), SOLVE_47, 1, (0, 1)),
+    ((14, 6), SOLVE_47, 2, (0, 1)),
+    ((30, 7), SOLVE_47, 3, (0, 1)),
 )
 BLOCK_SENDS = (
     ((3, 1), SOLVE_23, 0),
@@ -30,18 +32,23 @@
     ((7, 4), SOLVE_47, 2),
     ((7, 5), SOLVE_47, 3),
     ((7, 6), SOLVE_47, 4),
+    *(((5, c), (4, c), 0) for c in (2, 3)),
+    *(((6, c), (7, c), 0) for c in (2, 3)),
 )
 
+RIGHT_SENDS = (((3, 2), SOLVE_23), ((5, 3), (4, 3)), ((6, 3), (7, 3)))
+
 
 def special_pairs():
-    pairs = {(s, t) for s, t, _ in INVERSE_SENDS} | {(s, t) for s, t, _ in BLOCK_SENDS}
-    pairs |= {(SOLVE_1, (z, 1)) for z in range(N_Z)}
+    pairs = {(s, t) for s, t, _, _ in INVERSE_SENDS} | {(s, t) for s, t, _ in BLOCK_SENDS}
+    pairs |= {(SOLVE_0, (z, 0)) for z in (1, 2, 3)} | {(SOLVE_1, (z, 1)) for z in (0, 1, 2, 4, 5)}
+    pairs |= {((r, 1), (4 if r < 6 else 7, 3)) for r in range(4, 8)}
+    pairs |= {((3, 0), (4, 0)), ((0, 1), (5, 0))} | {((0, 1), (r, c)) for r in (6, 7) for c in (0, 1)}
     pairs |= {((3, 0), SOLVE_23)}
-    pairs |= {(SOLVE_23, (r, c)) for c in (2, 3) for r in (4, 5, 7)}
-    pairs |= {((7, c), (6, c)) for c in (2, 3)}
+    pairs |= {(SOLVE_23, (r, c)) for c in (2, 3) for r in (4, 7)}
     pairs |= {(SOLVE_23, (2, c)) for c in range(8) if c != 1}
     pairs |= {(SOLVE_47, (6, c)) for c in range(8) if c != 4}
-    pairs |= {((r, c), SOLVE_47) for c in (1, 3) for r in range(4, 8)}
+    pairs |= {((r, 3), SOLVE_47) for r in (4, 7)} | {((r, 0), (r, 3)) for r in (4, 7)} | {((r, 1), (r, 3)) for r in (4, 7)}
     pairs |= {(SOLVE_47, (r, 0)) for r in range(4, 8)}
     return sorted({tuple(sorted(p)) for p in pairs})
 
@@ -50,7 +57,7 @@
     lower, slab, inverses, out,
     panel, inv, inv_parts, blocks, right, right_own, x_own, x_stage, x_full, x_in,
     acc_f, acc_b, stage_f, stage_b, relays, pair_out, pair_in, sums, cross_in,
-    load_sem, send_sem, x_sem, x_in_sem, relay_sem, inv_sem, block_sem, acc_f_sem, acc_b_sem, pair_sem, cross_sem,
+    load_sem, send_sem, x_sem, x_in_sem, side_sem, go_sem, relay_sem, inv_sem, block_sem, acc_f_sem, acc_b_sem, pair_sem, cross_sem,
 ):
     row = lax.axis_index("row")
     col = lax.axis_index("col")
@@ -121,17 +128,18 @@
         greet((row, (x + d) % N_X * 2 + core))
     count = jnp.int32(N_X)
     is_root = (z == root_z) & (col < 2)
-
-    @pl.when(is_root)
+    in_other = (col < 2) & (y != 0)
+
+    @pl.when(is_root & in_other)
     def _():
         for d in range(1, N_Z):
             greet((y * N_Z + (z + d) % N_Z, col))
 
-    @pl.when((col < 2) & (z != root_z))
+    @pl.when(jnp.logical_not(is_root) & in_other)
     def _():
         greet((y * N_Z + root_z, col))
 
-    count += jnp.where(is_root, N_Z - 1, jnp.where(col < 2, 1, 0))
+    count += jnp.where(in_other, jnp.where(is_root, N_Z - 1, 1), 0)
     is_relay = (z == 2) | (z == 6)
     relay_z = jnp.where(col < 4, 2, 6)
 
@@ -198,11 +206,17 @@
         def _(source=source, solver=solver, slot=slot):
             send(source, lower.at[0], blocks.at[slot], 0, block_sem.at[slot], solver)
 
+    for source, target in RIGHT_SENDS:
+
+        @pl.when(here(source))
+        def _(source=source, target=target):
+            send(source, slab.at[0], acc_f.at[2], 1, acc_f_sem.at[2], target)
+
     def part(slot, piece, b):
         return inv_parts.at[slot, piece, pl.ds(b * quarter, quarter), pl.ds(0, (b + 1) * quarter)]
 
     is_source = here(INVERSE_SENDS[0][0])
-    for source, _, _ in INVERSE_SENDS[1:]:
+    for source, _, _, _ in INVERSE_SENDS[1:]:
         is_source |= here(source)
 
     @pl.when(is_source)
@@ -210,11 +224,11 @@
         load_inv.wait()
         split_inverse(0)
 
-    for source, solver, slot in INVERSE_SENDS:
+    for source, solver, slot, pieces in INVERSE_SENDS:
 
         @pl.when(here(source))
-        def _(source=source, solver=solver, slot=slot):
-            for piece in range(2):
+        def _(source=source, solver=solver, slot=slot, pieces=pieces):
+            for piece in pieces:
                 for b in range(4):
                     s = 1 + piece * 4 + b
                     send(source, part(0, piece, b), part(slot, piece, b), s, inv_sem.at[slot, piece, b], solver)
@@ -252,13 +266,15 @@
         x_full[0] = value
 
     column_root = [SOLVE_0, (1, 1)]
-    in_plane = [(1, 2, 3, 4, 5, 6, 7), ()]
+    in_plane = [(1, 3, 2), ()]
 
     def spread_from_root(c):
         when = column_root[c]
         root_row = column_root[c][0]
         for i, target in enumerate(in_plane[c][:1]):
             send(when, x_own, x_own, 9 + i, x_sem, (target, c))
+        if c == 0:
+            send(when, x_own, x_stage.at[0], 19, side_sem, (0, 1))
         for d in (2, 1, 3):
             send(when, x_own, x_own, 15 + d, x_sem, (d * N_Z + root_row, c))
         for i, target in enumerate(in_plane[c]):
@@ -278,39 +294,60 @@
         value = solve(0, right[...] - product(panel[0], x_own[...]))
         x_stage[0] = value.astype(BF16)
         x_full[0] = value
-        for i, target in enumerate((2, 3, 1, 4, 5, 6, 7, 0)):
-            send(SOLVE_1, x_stage.at[0], x_own, 9 + i, x_sem, (target, 1))
+        send(SOLVE_1, x_stage.at[0], x_own, 9, x_sem, (2, 1))
+        send(SOLVE_1, x_stage.at[0], x_own, 10, x_sem, (4, 1))
+        for i, target in enumerate((5, 0, 1)):
+            send(SOLVE_1, x_stage.at[0], x_own, 11 + i, x_sem, (target, 1))
 
     def rows_of(c, r0, r1):
         return plane_row(r0, r1) & (col == c)
 
-    @pl.when(rows_of(0, 2, 8))
-    def _():
-        load_right.wait()
-        load_first.wait()
-        arrived(x_own, x_sem)
-        stage_f[...] = right[...] - product(panel[0], x_own[...])
+    @pl.when(here((2, 0)))
+    def _():
+        load_first.wait()
+        arrived(x_own, x_sem)
+        stage_f[0] = product(panel[0], x_own[...])
+        send((2, 0), stage_f.at[0], acc_f.at[0], 19, acc_f_sem.at[0], sibling)
 
     @pl.when(here((3, 0)))
     def _():
-        send((3, 0), stage_f, acc_f.at[1], 19, acc_f_sem.at[1], SOLVE_23)
-
-    to_sibling = rows_of(0, 2, 8) & (row != 3)
-
-    @pl.when(to_sibling)
-    def _():
-        send(to_sibling, stage_f, acc_f.at[0], 19, acc_f_sem.at[0], sibling)
-
-    for r in range(4, 8):
+        load_first.wait()
+        arrived(x_own, x_sem)
+        stage_b[0] = product(panel[0], x_own[...]).astype(BF16)
+        send((3, 0), stage_b.at[0], acc_b.at[0], 19, acc_b_sem.at[0], SOLVE_23)
+        send((3, 0), x_own, x_own, 9, x_sem, (4, 0))
+
+    @pl.when(here((0, 1)))
+    def _():
+        arrived(x_stage.at[0], side_sem)
+        for i, r in enumerate((5, 6, 7)):
+            send((0, 1), x_stage.at[0], x_own, 9 + i, x_sem, (r, 0))
+        arrived(x_own, x_sem)
+        for i, r in enumerate((6, 7)):
+            send((0, 1), x_own, x_own, 12 + i, x_sem, (r, 1))
+
+    low_0 = rows_of(0, 4, 8)
+    low_1 = rows_of(1, 4, 8)
+
+    @pl.when(low_0)
+    def _():
+        load_first.wait()
+        arrived(x_own, x_sem)
+        stage_f[0] = product(panel[0], x_own[...])
+        send(low_0, stage_f.at[0], acc_f.at[0], 18, acc_f_sem.at[0], sibling)
+
+    @pl.when(low_1)
+    def _():
+        load_first.wait()
+        arrived(x_own, x_sem)
+        arrived(acc_f.at[0], acc_f_sem.at[0])
+        stage_b[0] = (acc_f[0] + product(panel[0], x_own[...])).astype(BF16)
+
+    for r, target, slot in ((4, 4, 0), (5, 4, 1), (6, 7, 1), (7, 7, 0)):
 
         @pl.when(here((r, 1)))
-        def _(r=r):
-            load_right.wait()
-            load_first.wait()
-            arrived(x_own, x_sem)
-            arrived(acc_f.at[0], acc_f_sem.at[0])
-            stage_f[...] = acc_f[0] - product(panel[0], x_own[...])
-            send((r, 1), stage_f, acc_f.at[r - 2], 19, acc_f_sem.at[r - 2], SOLVE_47)
+        def _(r=r, target=target, slot=slot):
+            send((r, 1), stage_b.at[0], acc_b.at[slot], 19, acc_b_sem.at[slot], (target, 3))
 
     def scatter(when, slot, k, s):
         solver = SOLVE_23 if k < 4 else SOLVE_47
@@ -349,7 +386,7 @@
                     send(lambda: place() & (y == 0), piece, piece, first + i, relay_sem.at[slot], device)
 
             for i, target in enumerate(other_z):
-                direct = (lambda target=target: (y != 0) | (target < 4)) if k < 4 else (lambda: True)
+                direct = (lambda target=target: (y != 0) | ((target != 4) & (target != 7))) if k < 4 else (lambda: True)
 
                 @pl.when(direct())
                 def _(i=i, target=target, direct=direct):
@@ -371,55 +408,64 @@
         load_first.wait()
         arrived(acc_f.at[0], acc_f_sem.at[0])
         arrived(x_own, x_sem)
-        total = acc_f[0] - product(panel[0], x_own[...])
+        total = right[...] - acc_f[0] - product(panel[0], x_own[...])
         inverse_arrived(0)
         value = solve(0, total)
         x_stage[0] = value.astype(BF16)
         x_full[0] = value
-        for i, r in enumerate((4, 5, 7)):
+        for i, r in enumerate((4, 7)):
             send(when, x_stage.at[0], x_own, 20 + i, x_sem, (r, 2))
         scatter(when, 0, 2, 26)
         arrived(blocks.at[0], block_sem.at[0])
-        arrived(acc_f.at[1], acc_f_sem.at[1])
-        stage_f[...] = acc_f[1] - product(blocks[0], x_own[...])
+        arrived(acc_f.at[2], acc_f_sem.at[2])
+        arrived(acc_b.at[0], acc_b_sem.at[0])
+        stage_f[0] = acc_f[2] - acc_b[0].astype(F32) - product(blocks[0], x_own[...])
         arrived(blocks.at[1], block_sem.at[1])
-        total = stage_f[...] - product(blocks[1], x_stage[0])
+        total = stage_f[0] - product(blocks[1], x_stage[0])
         inverse_arrived(1)
         value = solve(1, total)
         x_stage[1] = value.astype(BF16)
         x_full[1] = value
-        for i, r in enumerate((4, 5, 7)):
+        for i, r in enumerate((4, 7)):
             send(when, x_stage.at[1], x_own, 23 + i, x_sem, (r, 3))
         scatter(when, 1, 3, 29)
-        send(when, x_full.at[0], x_in, 36, x_in_sem, (2, 0))
-        send(when, x_full.at[1], x_in, 37, x_in_sem, (3, 0))
-
-    low_rows = rows_of(2, 4, 8)
-
-    def pass_on(c):
-        @pl.when(row == 7)
-        def _():
-            send((7, c), x_own, x_own, 9, x_sem, (6, c))
-
-    @pl.when(low_rows)
-    def _():
-        load_first.wait()
-        arrived(x_own, x_sem)
-        pass_on(2)
-        stage_f[...] = product(panel[0], x_own[...])
-        send(low_rows, stage_f, acc_f.at[0], 19, acc_f_sem.at[0], sibling)
-
-    for r in range(4, 8):
+        send(when, x_own, x_own, 33, x_sem, (3, 1))
+
+    low_rows = (row == 4) | (row == 7)
+    low_2 = low_rows & (col == 2)
+
+    @pl.when(low_2)
+    def _():
+        load_first.wait()
+        arrived(x_own, x_sem)
+        stage_f[0] = product(panel[0], x_own[...])
+        send(low_2, stage_f.at[0], acc_f.at[0], 18, acc_f_sem.at[0], sibling)
+        arrived(blocks.at[0], block_sem.at[0])
+        stage_f[1] = product(blocks[0], x_own[...])
+        send(low_2, stage_f.at[1], acc_f.at[1], 19, acc_f_sem.at[1], sibling)
+
+    for r, rows in ((4, (4, 5)), (7, (6, 7))):
 
         @pl.when(here((r, 3)))
-        def _(r=r):
+        def _(r=r, rows=rows):
             load_first.wait()
-            arrived(x_own, x_sem)
-            if r == 7:
-                pass_on(3)
-            arrived(acc_f.at[0], acc_f_sem.at[0])
-            stage_b[...] = (acc_f[0] + product(panel[0], x_own[...])).astype(BF16)
-            send((r, 3), stage_b, acc_b.at[r - 4], 19, acc_b_sem.at[r - 4], SOLVE_47)
+            load_right.wait()
+            for i, target in enumerate(rows):
+                j = 0 if target == r else 1
+                if j == 1:
+                    arrived(acc_f.at[2], acc_f_sem.at[2])
+                    arrived(blocks.at[0], block_sem.at[0])
+                arrived(acc_b.at[j], acc_b_sem.at[j])
+                arrived(acc_f.at[j], acc_f_sem.at[j])
+                start = acc_f[2] if j == 1 else right[...]
+                stage_f[j] = start - acc_b[j].astype(F32) - acc_f[j]
+                if i == 0:
+                    arrived(x_own, x_sem)
+                    for c in (0, 1):
+                        pl.semaphore_signal(go_sem, inc=1, device_id=(r, c), device_id_type=MESH)
+                block = panel[0] if target == r else blocks[0]
+                stage_b[i] = (stage_f[j] - product(block, x_own[...])).astype(BF16)
+                send((r, 3), stage_b.at[i], acc_b.at[target - 4], 18 + i, acc_b_sem.at[target - 4], SOLVE_47)
 
     @pl.when(here(SOLVE_47))
     def _():
@@ -435,25 +481,26 @@
         for slot in range(1, 4):
             inverse_arrived(slot)
         for q in range(4):
-            arrived(acc_f.at[q + 2], acc_f_sem.at[q + 2])
             for j in range(q - 1):
-                acc_f[q + 2] -= product(place[q, j][...], x_stage[j])
-            total = acc_f[q + 2]
+                done = product(place[q, j][...], x_stage[j])
+                acc_f[q] = done if j == 0 else acc_f[q] + done
+            arrived(acc_b.at[q], acc_b_sem.at[q])
+            total = acc_b[q].astype(F32)
+            if q > 1:
+                total -= acc_f[q]
             if q > 0:
                 total -= product(place[q, q - 1][...], x_stage[q - 1])
-            arrived(acc_b.at[q], acc_b_sem.at[q])
-            total -= acc_b[q].astype(F32)
             value = solve(q, total)
             x_stage[q] = value.astype(BF16)
             x_full[q] = value
             scatter(when, q, 4 + q, 20 + 4 * q)
-        for q in range(4):
-            send(when, x_full.at[q], x_in, 36 + q, x_in_sem, (4 + q, 0))
-
+            if q < 2:
+                send(when, x_full.at[q], x_in, 36 + q, x_in_sem, (4 + q, 0))
+        send(when, x_full.at[2], x_in, 38, x_in_sem, (6, 0))
     for k in range(2, 8):
         relay_quarter(k)
 
-    waited = rows_of(0, 0, 8) | (plane_row(4, 8) & (col < 4)) | here(SOLVE_23)
+    waited = rows_of(0, 0, 8) | here((0, 1)) | low_1 | (low_rows & (col < 4)) | here(SOLVE_23)
 
     @pl.when(jnp.logical_not(waited) & (col < 2))
     def _():
@@ -482,9 +529,8 @@
             send(relay, x_own, x_own, 9 + i, x_sem, peer)
 
     always = row >= 0
-    waited_first = (plane_row(2, 8) & (col < 4)) | here(SOLVE_1) | here(SOLVE_47)
-    waited_first = waited_first & jnp.logical_not((col > 1) & (row < 4)) & jnp.logical_not(here((2, 1)))
-    waited_first = waited_first & jnp.logical_not(here((3, 1))) | here(SOLVE_23)
+    waited_first = rows_of(0, 2, 8) | low_1 | (low_rows & (col < 4))
+    waited_first = waited_first | here(SOLVE_1) | here(SOLVE_23) | here(SOLVE_47)
 
     @pl.when(jnp.logical_not(waited_first))
     def _():
@@ -492,20 +538,34 @@
 
     load_rest.wait()
     value = x_own[...]
-    for i in range(4):
-        pair_out[i] = product(panel[2 * i + 1 - core], value).astype(BF16)
-    send(always, pair_out, pair_in, 64, pair_sem, sibling)
-    for i in range(4):
-        sums[i] = product(panel[2 * i + core], value).astype(BF16)
-    arrived(pair_in, pair_sem)
-    for i in range(4):
-        sums[i] = (sums[i].astype(F32) + pair_in[i].astype(F32)).astype(BF16)
-    for d in (2, 1, 3):
-        owner = (x + d) % N_X
-        send(always, sums.at[owner], cross_in.at[d - 1], 64 + d, cross_sem.at[d - 1], (row, owner * 2 + core))
+    distances = (2, 1, 3, 0)
+    owners = [(x + d) % N_X for d in distances]
+    for j, owner in enumerate(owners):
+        pair_out[j] = product(panel[2 * owner + 1 - core], value).astype(BF16)
+        send(always, pair_out.at[j], pair_in.at[j], 64 + j, pair_sem.at[j], sibling)
+
+    @pl.when(low_rows & (col < 2))
+    def _():
+        pl.semaphore_wait(go_sem, 1)
+
+    for j, (d, owner) in enumerate(zip(distances, owners)):
+        total = product(panel[2 * owner + core], value)
+        arrived(pair_in.at[j], pair_sem.at[j])
+        total = total + pair_in[j].astype(F32)
+        if d > 0:
+            sums[j] = total.astype(BF16)
+            send(always, sums.at[j], cross_in.at[d - 1], 68 + j, cross_sem.at[d - 1], (row, owner * 2 + core))
+    @pl.when(here(SOLVE_23))
+    def _():
+        for q in range(2):
+            send(SOLVE_23, x_full.at[q], x_in, 36 + q, x_in_sem, (2 + q, 0))
+
+    @pl.when(here(SOLVE_47))
+    def _():
+        send(SOLVE_47, x_full.at[3], x_in, 39, x_in_sem, (7, 0))
 
     load_own.wait()
-    total = right_own[...] - sums[x].astype(F32)
+    total = right_own[...] - total
     for d in range(3):
         arrived(cross_in.at[d], cross_sem.at[d])
         total -= cross_in[d].astype(F32)
@@ -526,14 +586,13 @@
     def _():
         load_inv.wait()
 
-    read_right = plane_row(2, 8) & (col == 0) | plane_row(4, 8) & (col == 1)
-    read_right = read_right | here(SOLVE_0) | here(SOLVE_1) | here(SOLVE_23) | here(SOLVE_47)
+    read_right = here(SOLVE_0) | here(SOLVE_1) | here(SOLVE_23) | here(SOLVE_47) | (low_rows & (col == 3))
 
     @pl.when(jnp.logical_not(read_right))
     def _():
         load_right.wait()
 
-    buffers = [x_own, stage_f, pair_out, relays.at[0]]
+    buffers = [x_own, stage_f.at[0], relays.at[0]]
 
     def same_size(shape, dtype):
         for buffer in buffers:
@@ -567,25 +626,27 @@
         vmem((4, order, width), BF16),
         vmem((4, order, width), F32),
         vmem((order, width), F32),
-        vmem((6, order, width), F32),
+        vmem((4, order, width), F32),
         vmem((4, order, width), BF16),
-        vmem((order, width), F32),
-        vmem((order, width), BF16),
+        vmem((2, order, width), F32),
+        vmem((2, order, width), BF16),
         vmem((2, order // 4, width), BF16),
         vmem((4, order, width), BF16),
         vmem((4, order, width), BF16),
-        vmem((4, order, width), BF16),
+        vmem((3, order, width), BF16),
         vmem((3, order, width), BF16),
         dma((5,)),
         dma((72,)),
         dma,
         dma,
+        dma,
+        pltpu.SemaphoreType.REGULAR,
         dma((2,)),
         dma((4, 2, 4)),
         dma((5,)),
-        dma((6,)),
         dma((4,)),
-        dma,
+        dma((4,)),
+        dma((4,)),
         dma((3,)),
     ]
     result = pl.pallas_call(
@@ -596,7 +657,7 @@
         out_specs=pl.BlockSpec(memory_space=pltpu.VMEM),
         scratch_shapes=scratch,
         compiler_params=pltpu.CompilerParams(
-            collective_id=0, has_side_effects=True, vmem_limit_bytes=60 << 20
+            collective_id=0, has_side_effects=True, vmem_limit_bytes=53 << 20
         ),
     )(
         lower.reshape(row_blocks, order, order),

time: 64.9 us -> 59.1 us (0.911)
  Pallas kernels: 63.2 us -> 58.2 us
  local copies, waits for them, and re-layouts: 1.67 us -> 0.71 us
    pallas_call x1, Pallas kernels: 63.2 us -> 58.2 us  [body(): pl.pallas_call(kernel, name='window_solve', out_shape=jax.ShapeDtypeStruc...]
    unnamed x1, local copies, waits for them, and re-layouts: 1.67 us -> 0.71 us
where the time goes in v3:
time: 59.1 us; the launch traced here: 58.9 us
  Pallas kernels  58.2 us (98%)
  local copies, waits for them, and re-layouts  0.71 us (1%)
    pallas_call x1, Pallas kernels, body(): pl.pallas_call(kernel, name='window_solve', out_shape=jax.ShapeDtypeStruc...  58.2 us

profile of v3, /device:TPU:21, one launch (start us, length us, event | category | flops | bytes accessed | tf_op | source)
XLA Modules:
  0.0 58.9 jit_solution(6463154588572176806)
XLA Ops:
  0.0 58.2 %window_solve.1 = f32[512,128]{1,0:T(8,128)S(1)} custom-call(bf16[8,512,512]{2,1,0:T(8,128)(2,1)} %bitcast.5, f32[8,512,128]{2,1,0:T(8,128)} %bitcast.6, f32[512,512]{1,0:T(8,128)} %bitcast.7), custom_call_target="tpu_custom_call" | custom-call | tf_op jit(solution)/shard_map/window_solve/pallas_call | solution.py:652
  58.2 0.7 %copy.5 = f32[1,1,512,128]{3,2,1,0:T(8,128)} copy(f32[1,1,512,128]{3,2,1,0:T(8,128)S(1)} %bitcast.4) | data formatting | bytes 524288

commit v4 on v3

--- a/solution.py
+++ b/solution.py
@@ -14,15 +14,17 @@
 SOLVE_1 = (1, 0)
 SOLVE_23 = (2, 1)
 SOLVE_47 = (6, 4)
+HIGH = tuple((0, b) for b in range(4))
+LOW = tuple((1, b) for b in range(4))
 INVERSE_SENDS = (
-    ((1, 1), SOLVE_1, 0, (0, 1)),
-    ((9, 2), SOLVE_23, 0, (0,)),
-    ((25, 2), SOLVE_23, 0, (1,)),
-    ((12, 3), SOLVE_23, 1, (0,)),
-    ((28, 3), SOLVE_23, 1, (1,)),
-    ((6, 5), SOLVE_47, 1, (0, 1)),
-    ((14, 6), SOLVE_47, 2, (0, 1)),
-    ((30, 7), SOLVE_47, 3, (0, 1)),
+    ((1, 1), SOLVE_1, 0, HIGH + LOW),
+    ((9, 2), SOLVE_23, 0, (HIGH[0], HIGH[3])),
+    ((25, 2), SOLVE_23, 0, (HIGH[1], HIGH[2])),
+    ((12, 3), SOLVE_23, 1, (HIGH[0], HIGH[3])),
+    ((28, 3), SOLVE_23, 1, (HIGH[1], HIGH[2])),
+    ((6, 5), SOLVE_47, 1, HIGH),
+    ((14, 6), SOLVE_47, 2, HIGH),
+    ((30, 7), SOLVE_47, 3, HIGH),
 )
 BLOCK_SENDS = (
     ((3, 1), SOLVE_23, 0),
@@ -36,8 +38,6 @@
     *(((6, c), (7, c), 0) for c in (2, 3)),
 )
 
-RIGHT_SENDS = (((3, 2), SOLVE_23), ((5, 3), (4, 3)), ((6, 3), (7, 3)))
-
 
 def special_pairs():
     pairs = {(s, t) for s, t, _, _ in INVERSE_SENDS} | {(s, t) for s, t, _ in BLOCK_SENDS}
@@ -48,7 +48,7 @@
     pairs |= {(SOLVE_23, (r, c)) for c in (2, 3) for r in (4, 7)}
     pairs |= {(SOLVE_23, (2, c)) for c in range(8) if c != 1}
     pairs |= {(SOLVE_47, (6, c)) for c in range(8) if c != 4}
-    pairs |= {((r, 3), SOLVE_47) for r in (4, 7)} | {((r, 0), (r, 3)) for r in (4, 7)} | {((r, 1), (r, 3)) for r in (4, 7)}
+    pairs |= {((4, 3), (7, 3))} | {((r, 3), SOLVE_47) for r in (4, 7)} | {((r, 0), (r, 3)) for r in (4, 7)} | {((r, 1), (r, 3)) for r in (4, 7)}
     pairs |= {(SOLVE_47, (r, 0)) for r in range(4, 8)}
     return sorted({tuple(sorted(p)) for p in pairs})
 
@@ -97,8 +97,6 @@
     load_inv.start()
     load_right.start()
     load_first.start()
-    load_rest.start()
-    load_own.start()
 
     def clear_slot(slot):
         inv_parts[slot] = jnp.zeros(inv_parts.shape[1:], BF16)
@@ -192,78 +190,72 @@
             for other in others:
                 greet(other)
 
-    pl.semaphore_wait(barrier, count)
-
     def split_inverse(slot):
         value = inv[...]
         high = value.astype(BF16)
         inv_parts[slot, 0] = high
         inv_parts[slot, 1] = (value - high.astype(F32)).astype(BF16)
 
+    def part(slot, piece, b):
+        return inv_parts.at[slot, piece, pl.ds(b * quarter, quarter), pl.ds(0, (b + 1) * quarter)]
+
+    def inverse_arrived(slot, parts=HIGH):
+        for piece, b in parts:
+            arrived(part(slot, piece, b), inv_sem.at[slot, piece, b])
+
+    def solve(slot, total, low_part=False):
+        high = total.astype(BF16)
+        low = (total - high.astype(F32)).astype(BF16)
+        both = jnp.concatenate([high, low], axis=1)
+
+        def times(rows, depth):
+            done = jnp.dot(inv_parts[slot, 0, rows, :depth], both[:depth], preferred_element_type=F32)
+            if low_part:
+                done += jnp.dot(inv_parts[slot, 1, rows, :depth], both[:depth], preferred_element_type=F32)
+            return done
+
+        whole = jnp.concatenate([times(slice(0, half), half), times(slice(half, 2 * half), 2 * half)], axis=0)
+        return whole[:, :width] + whole[:, width:]
+
+    def product(block, value):
+        return jnp.dot(block, value, preferred_element_type=F32)
+
+    is_source = here(INVERSE_SENDS[0][0])
+    for source, _, _, _ in INVERSE_SENDS[1:]:
+        is_source |= here(source)
+
+    @pl.when(is_source)
+    def _():
+        load_inv.wait()
+        split_inverse(0)
+
+    @pl.when(here(SOLVE_0))
+    def _():
+        load_inv.wait()
+        split_inverse(0)
+        load_right.wait()
+        value = solve(0, right[...], low_part=True)
+        x_own[...] = value.astype(BF16)
+        x_full[0] = value
+
+    pl.semaphore_wait(barrier, count)
+
+    load_rest.start()
+    load_own.start()
+
     for source, solver, slot in BLOCK_SENDS:
 
         @pl.when(here(source))
         def _(source=source, solver=solver, slot=slot):
             send(source, lower.at[0], blocks.at[slot], 0, block_sem.at[slot], solver)
 
-    for source, target in RIGHT_SENDS:
-
-        @pl.when(here(source))
-        def _(source=source, target=target):
-            send(source, slab.at[0], acc_f.at[2], 1, acc_f_sem.at[2], target)
-
-    def part(slot, piece, b):
-        return inv_parts.at[slot, piece, pl.ds(b * quarter, quarter), pl.ds(0, (b + 1) * quarter)]
-
-    is_source = here(INVERSE_SENDS[0][0])
-    for source, _, _, _ in INVERSE_SENDS[1:]:
-        is_source |= here(source)
-
-    @pl.when(is_source)
-    def _():
-        load_inv.wait()
-        split_inverse(0)
-
     for source, solver, slot, pieces in INVERSE_SENDS:
 
         @pl.when(here(source))
         def _(source=source, solver=solver, slot=slot, pieces=pieces):
-            for piece in pieces:
-                for b in range(4):
-                    s = 1 + piece * 4 + b
-                    send(source, part(0, piece, b), part(slot, piece, b), s, inv_sem.at[slot, piece, b], solver)
-
-    def inverse_arrived(slot):
-        for piece in range(2):
-            for b in range(4):
-                arrived(part(slot, piece, b), inv_sem.at[slot, piece, b])
-
-    def solve(slot, total):
-        high = total.astype(BF16)
-        low = (total - high.astype(F32)).astype(BF16)
-        both = jnp.concatenate([high, low], axis=1)
-
-        def times(rows, depth):
-            a = inv_parts[slot, 0, rows, :depth]
-            b = inv_parts[slot, 1, rows, :depth]
-            return jnp.dot(a, both[:depth], preferred_element_type=F32) + jnp.dot(
-                b, both[:depth], preferred_element_type=F32
-            )
-
-        whole = jnp.concatenate([times(slice(0, half), half), times(slice(half, 2 * half), 2 * half)], axis=0)
-        return whole[:, :width] + whole[:, width:]
-
-    def product(block, value):
-        return jnp.dot(block, value, preferred_element_type=F32)
-
-    @pl.when(here(SOLVE_0))
-    def _():
-        load_inv.wait()
-        split_inverse(0)
-        load_right.wait()
-        value = solve(0, right[...])
-        x_own[...] = value.astype(BF16)
-        x_full[0] = value
+            for piece, b in pieces:
+                s = 1 + piece * 4 + b
+                send(source, part(0, piece, b), part(slot, piece, b), s, inv_sem.at[slot, piece, b], solver)
 
     column_root = [SOLVE_0, (1, 1)]
     in_plane = [(1, 3, 2), ()]
@@ -289,9 +281,9 @@
     def _():
         load_right.wait()
         load_first.wait()
-        inverse_arrived(0)
-        arrived(x_own, x_sem)
-        value = solve(0, right[...] - product(panel[0], x_own[...]))
+        inverse_arrived(0, HIGH + LOW)
+        arrived(x_own, x_sem)
+        value = solve(0, right[...] - product(panel[0], x_own[...]), low_part=True)
         x_stage[0] = value.astype(BF16)
         x_full[0] = value
         send(SOLVE_1, x_stage.at[0], x_own, 9, x_sem, (2, 1))
@@ -311,9 +303,10 @@
 
     @pl.when(here((3, 0)))
     def _():
-        load_first.wait()
-        arrived(x_own, x_sem)
-        stage_b[0] = product(panel[0], x_own[...]).astype(BF16)
+        load_right.wait()
+        load_first.wait()
+        arrived(x_own, x_sem)
+        stage_b[0] = (right[...] - product(panel[0], x_own[...])).astype(BF16)
         send((3, 0), stage_b.at[0], acc_b.at[0], 19, acc_b_sem.at[0], SOLVE_23)
         send((3, 0), x_own, x_own, 9, x_sem, (4, 0))
 
@@ -340,8 +333,9 @@
     def _():
         load_first.wait()
         arrived(x_own, x_sem)
+        load_right.wait()
         arrived(acc_f.at[0], acc_f_sem.at[0])
-        stage_b[0] = (acc_f[0] + product(panel[0], x_own[...])).astype(BF16)
+        stage_b[0] = (right[...] - acc_f[0] - product(panel[0], x_own[...])).astype(BF16)
 
     for r, target, slot in ((4, 4, 0), (5, 4, 1), (6, 7, 1), (7, 7, 0)):
 
@@ -359,7 +353,7 @@
 
     own_rows = pl.ds(pl.multiple_of(x * quarter, quarter), quarter)
     other_planes = [(d * N_Z + z, col) for d in range(1, N_Y)]
-    other_z = [y * N_Z + (z + d) % N_Z for d in (4, 3, 5, 2, 6, 1, 7)]
+    other_z = [y * N_Z + (z + d) % N_Z for d in (2, 3, 4, 5, 1, 6, 7)]
 
     def relay_quarter(k):
         solver = SOLVE_23 if k < 4 else SOLVE_47
@@ -417,9 +411,8 @@
             send(when, x_stage.at[0], x_own, 20 + i, x_sem, (r, 2))
         scatter(when, 0, 2, 26)
         arrived(blocks.at[0], block_sem.at[0])
-        arrived(acc_f.at[2], acc_f_sem.at[2])
         arrived(acc_b.at[0], acc_b_sem.at[0])
-        stage_f[0] = acc_f[2] - acc_b[0].astype(F32) - product(blocks[0], x_own[...])
+        stage_f[0] = acc_b[0].astype(F32) - product(blocks[0], x_own[...])
         arrived(blocks.at[1], block_sem.at[1])
         total = stage_f[0] - product(blocks[1], x_stage[0])
         inverse_arrived(1)
@@ -449,23 +442,24 @@
         @pl.when(here((r, 3)))
         def _(r=r, rows=rows):
             load_first.wait()
-            load_right.wait()
             for i, target in enumerate(rows):
                 j = 0 if target == r else 1
                 if j == 1:
-                    arrived(acc_f.at[2], acc_f_sem.at[2])
                     arrived(blocks.at[0], block_sem.at[0])
                 arrived(acc_b.at[j], acc_b_sem.at[j])
                 arrived(acc_f.at[j], acc_f_sem.at[j])
-                start = acc_f[2] if j == 1 else right[...]
-                stage_f[j] = start - acc_b[j].astype(F32) - acc_f[j]
+                stage_f[j] = acc_b[j].astype(F32) - acc_f[j]
                 if i == 0:
                     arrived(x_own, x_sem)
                     for c in (0, 1):
                         pl.semaphore_signal(go_sem, inc=1, device_id=(r, c), device_id_type=MESH)
                 block = panel[0] if target == r else blocks[0]
                 stage_b[i] = (stage_f[j] - product(block, x_own[...])).astype(BF16)
+                if target == 6:
+                    pl.semaphore_wait(go_sem, 1)
                 send((r, 3), stage_b.at[i], acc_b.at[target - 4], 18 + i, acc_b_sem.at[target - 4], SOLVE_47)
+                if target == 5:
+                    pl.semaphore_signal(go_sem, inc=1, device_id=(7, 3), device_id_type=MESH)
 
     @pl.when(here(SOLVE_47))
     def _():
@@ -586,7 +580,7 @@
     def _():
         load_inv.wait()
 
-    read_right = here(SOLVE_0) | here(SOLVE_1) | here(SOLVE_23) | here(SOLVE_47) | (low_rows & (col == 3))
+    read_right = here((3, 0)) | here(SOLVE_0) | here(SOLVE_1) | here(SOLVE_23) | here(SOLVE_47) | low_1
 
     @pl.when(jnp.logical_not(read_right))
     def _():

time: 59.1 us -> 55.6 us (0.941); the launches traced: 58.9 us -> 54.8 us
  Pallas kernels: 58.2 us -> 54.1 us
    pallas_call x1, Pallas kernels: 58.2 us -> 54.1 us  [body(): pl.pallas_call(kernel, name='window_solve', out_shape=jax.ShapeDtypeStruc...]
where the time goes in v4:
time: 55.6 us; the launch traced here: 54.8 us
  Pallas kernels  54.1 us (97%)
  local copies, waits for them, and re-layouts  0.71 us (1%)
    pallas_call x1, Pallas kernels, body(): pl.pallas_call(kernel, name='window_solve', out_shape=jax.ShapeDtypeStruc...  54.1 us

profile of v4, /device:TPU:21, one launch (start us, length us, event | category | flops | bytes accessed | tf_op | source)
XLA Modules:
  0.0 54.8 jit_solution(8329110365955278748)
XLA Ops:
  0.0 54.1 %window_solve.1 = f32[512,128]{1,0:T(8,128)S(1)} custom-call(bf16[8,512,512]{2,1,0:T(8,128)(2,1)} %bitcast.5, f32[8,512,128]{2,1,0:T(8,128)} %bitcast.6, f32[512,512]{1,0:T(8,128)} %bitcast.7), custom_call_target="tpu_custom_call" | custom-call | tf_op jit(solution)/shard_map/window_solve/pallas_call | solution.py:646
  54.1 0.7 %copy.5 = f32[1,1,512,128]{3,2,1,0:T(8,128)} copy(f32[1,1,512,128]{3,2,1,0:T(8,128)S(1)} %bitcast.4) | data formatting | bytes 524288

commit v5 on v4

--- a/solution.py
+++ b/solution.py
@@ -55,15 +55,15 @@
 
 def kernel(
     lower, slab, inverses, out,
-    panel, inv, inv_parts, blocks, right, right_own, x_own, x_stage, x_full, x_in,
-    acc_f, acc_b, stage_f, stage_b, relays, pair_out, pair_in, sums, cross_in,
-    load_sem, send_sem, x_sem, x_in_sem, side_sem, go_sem, relay_sem, inv_sem, block_sem, acc_f_sem, acc_b_sem, pair_sem, cross_sem,
+    first, panel, inv, inv_parts, blocks, right, right_own, x_own, x_stage, x_full, x_in,
+    acc_f, acc_b, stage_f, stage_b, relays, x_mate, ours, sums, cross_in,
+    load_sem, send_sem, x_sem, x_in_sem, side_sem, go_sem, relay_sem, inv_sem, block_sem, acc_f_sem, acc_b_sem, mate_sem, cross_sem,
 ):
     row = lax.axis_index("row")
     col = lax.axis_index("col")
     y, z = row // N_Z, row % N_Z
     x, core = col // 2, col % 2
-    half = panel.shape[1] // 2
+    half = first.shape[0] // 2
     quarter = half // 2
     width = x_own.shape[1]
 
@@ -76,6 +76,7 @@
     root_z = col
     sibling = (row, col + 1 - 2 * core)
     pending = []
+    relay_waits = {}
 
     def remote(src, dst, s, recv, device):
         return pltpu.make_async_remote_copy(
@@ -84,13 +85,14 @@
 
     def send(when, src, dst, s, recv, device):
         remote(src, dst, s, recv, device).start()
-        pending.append((when, s, src.shape, src.dtype))
+        if when is not None:
+            pending.append((when, s, src.shape, src.dtype))
 
     def arrived(dst, recv):
         remote(dst, dst, 0, recv, sibling).wait_recv()
 
-    load_first = pltpu.make_async_copy(lower.at[0], panel.at[0], load_sem.at[0])
-    load_rest = pltpu.make_async_copy(lower.at[pl.ds(1, 7)], panel.at[pl.ds(1, 7)], load_sem.at[1])
+    load_first = pltpu.make_async_copy(lower.at[0, 0], first, load_sem.at[0])
+    load_ours = pltpu.make_async_copy(lower.at[:, core], panel.at[0], load_sem.at[1])
     load_inv = pltpu.make_async_copy(inverses, inv, load_sem.at[2])
     load_right = pltpu.make_async_copy(slab.at[0], right, load_sem.at[3])
     load_own = pltpu.make_async_copy(slab.at[col], right_own, load_sem.at[4])
@@ -182,13 +184,32 @@
     for a, b in special_pairs():
         partners.setdefault(a, []).append(b)
         partners.setdefault(b, []).append(a)
+    by_row = {}
     for device, others in partners.items():
         count += jnp.where(here(device), len(others), 0)
-
-        @pl.when(here(device))
-        def _(others=others):
-            for other in others:
-                greet(other)
+        by_row.setdefault(device[0], []).append((device[1], others))
+
+    def greet_row(r):
+        @pl.when(row == r)
+        def _():
+            for c, others in by_row[r]:
+
+                @pl.when(col == c)
+                def _(others=others):
+                    for other in others:
+                        greet(other)
+
+    @pl.when(y == 0)
+    def _():
+        for r in by_row:
+            if r < N_Z:
+                greet_row(r)
+
+    @pl.when(y != 0)
+    def _():
+        for r in by_row:
+            if r >= N_Z:
+                greet_row(r)
 
     def split_inverse(slot):
         value = inv[...]
@@ -240,14 +261,14 @@
 
     pl.semaphore_wait(barrier, count)
 
-    load_rest.start()
+    load_ours.start()
     load_own.start()
 
     for source, solver, slot in BLOCK_SENDS:
 
         @pl.when(here(source))
         def _(source=source, solver=solver, slot=slot):
-            send(source, lower.at[0], blocks.at[slot], 0, block_sem.at[slot], solver)
+            send(source, lower.at[0, 0], blocks.at[slot], 0, block_sem.at[slot], solver)
 
     for source, solver, slot, pieces in INVERSE_SENDS:
 
@@ -256,6 +277,8 @@
             for piece, b in pieces:
                 s = 1 + piece * 4 + b
                 send(source, part(0, piece, b), part(slot, piece, b), s, inv_sem.at[slot, piece, b], solver)
+
+    remote(lower.at[:, 1 - core], panel.at[1], 65, mate_sem.at[1], sibling).start()
 
     column_root = [SOLVE_0, (1, 1)]
     in_plane = [(1, 3, 2), ()]
@@ -283,7 +306,7 @@
         load_first.wait()
         inverse_arrived(0, HIGH + LOW)
         arrived(x_own, x_sem)
-        value = solve(0, right[...] - product(panel[0], x_own[...]), low_part=True)
+        value = solve(0, right[...] - product(first[...], x_own[...]), low_part=True)
         x_stage[0] = value.astype(BF16)
         x_full[0] = value
         send(SOLVE_1, x_stage.at[0], x_own, 9, x_sem, (2, 1))
@@ -298,7 +321,7 @@
     def _():
         load_first.wait()
         arrived(x_own, x_sem)
-        stage_f[0] = product(panel[0], x_own[...])
+        stage_f[0] = product(first[...], x_own[...])
         send((2, 0), stage_f.at[0], acc_f.at[0], 19, acc_f_sem.at[0], sibling)
 
     @pl.when(here((3, 0)))
@@ -306,7 +329,7 @@
         load_right.wait()
         load_first.wait()
         arrived(x_own, x_sem)
-        stage_b[0] = (right[...] - product(panel[0], x_own[...])).astype(BF16)
+        stage_b[0] = (right[...] - product(first[...], x_own[...])).astype(BF16)
         send((3, 0), stage_b.at[0], acc_b.at[0], 19, acc_b_sem.at[0], SOLVE_23)
         send((3, 0), x_own, x_own, 9, x_sem, (4, 0))
 
@@ -326,7 +349,7 @@
     def _():
         load_first.wait()
         arrived(x_own, x_sem)
-        stage_f[0] = product(panel[0], x_own[...])
+        stage_f[0] = product(first[...], x_own[...])
         send(low_0, stage_f.at[0], acc_f.at[0], 18, acc_f_sem.at[0], sibling)
 
     @pl.when(low_1)
@@ -335,7 +358,7 @@
         arrived(x_own, x_sem)
         load_right.wait()
         arrived(acc_f.at[0], acc_f_sem.at[0])
-        stage_b[0] = (right[...] - acc_f[0] - product(panel[0], x_own[...])).astype(BF16)
+        stage_b[0] = (right[...] - acc_f[0] - product(first[...], x_own[...])).astype(BF16)
 
     for r, target, slot in ((4, 4, 0), (5, 4, 1), (6, 7, 1), (7, 7, 0)):
 
@@ -359,7 +382,8 @@
         solver = SOLVE_23 if k < 4 else SOLVE_47
         slot = max(k // 2 - 2, 0)
         piece = relays.at[slot]
-        first = 40 + 12 * slot
+        base = 40 + 12 * slot
+        waits = relay_waits.setdefault(k, [])
 
         place = lambda: (z == solver[0]) & (core == k % 2)
 
@@ -377,15 +401,16 @@
             @pl.when(y == 0)
             def _():
                 for i, device in enumerate(other_planes):
-                    send(lambda: place() & (y == 0), piece, piece, first + i, relay_sem.at[slot], device)
+                    send(None, piece, piece, base + i, relay_sem.at[slot], device)
+                    waits.append((lambda: y == 0, base + i))
 
             for i, target in enumerate(other_z):
                 direct = (lambda target=target: (y != 0) | ((target != 4) & (target != 7))) if k < 4 else (lambda: True)
 
                 @pl.when(direct())
                 def _(i=i, target=target, direct=direct):
-                    wanted = lambda: place() & direct()
-                    send(wanted, piece, x_own.at[own_rows], first + 3 + i, x_sem, (target, k))
+                    waits.append((direct, base + 3 + i))
+                    send(None, piece, x_own.at[own_rows], base + 3 + i, x_sem, (target, k))
 
             @pl.when(col == k)
             def _():
@@ -393,7 +418,8 @@
 
             @pl.when(col != k)
             def _():
-                send(lambda: place() & (col != k), piece, x_own.at[own_rows], first + 10, x_sem, (row, k))
+                waits.append((lambda: col != k, base + 10))
+                send(None, piece, x_own.at[own_rows], base + 10, x_sem, (row, k))
 
     @pl.when(here(SOLVE_23))
     def _():
@@ -402,7 +428,7 @@
         load_first.wait()
         arrived(acc_f.at[0], acc_f_sem.at[0])
         arrived(x_own, x_sem)
-        total = right[...] - acc_f[0] - product(panel[0], x_own[...])
+        total = right[...] - acc_f[0] - product(first[...], x_own[...])
         inverse_arrived(0)
         value = solve(0, total)
         x_stage[0] = value.astype(BF16)
@@ -431,7 +457,7 @@
     def _():
         load_first.wait()
         arrived(x_own, x_sem)
-        stage_f[0] = product(panel[0], x_own[...])
+        stage_f[0] = product(first[...], x_own[...])
         send(low_2, stage_f.at[0], acc_f.at[0], 18, acc_f_sem.at[0], sibling)
         arrived(blocks.at[0], block_sem.at[0])
         stage_f[1] = product(blocks[0], x_own[...])
@@ -453,7 +479,7 @@
                     arrived(x_own, x_sem)
                     for c in (0, 1):
                         pl.semaphore_signal(go_sem, inc=1, device_id=(r, c), device_id_type=MESH)
-                block = panel[0] if target == r else blocks[0]
+                block = first[...] if target == r else blocks[0]
                 stage_b[i] = (stage_f[j] - product(block, x_own[...])).astype(BF16)
                 if target == 6:
                     pl.semaphore_wait(go_sem, 1)
@@ -468,7 +494,7 @@
         split_inverse(0)
         load_first.wait()
         load_right.wait()
-        place = {(1, 0): blocks.at[0], (2, 0): panel.at[0], (2, 1): blocks.at[1]}
+        place = {(1, 0): blocks.at[0], (2, 0): first, (2, 1): blocks.at[1]}
         place |= {(3, 0): blocks.at[2], (3, 1): blocks.at[3], (3, 2): blocks.at[4]}
         for slot in range(5):
             arrived(blocks.at[slot], block_sem.at[slot])
@@ -530,22 +556,21 @@
     def _():
         load_first.wait()
 
-    load_rest.wait()
-    value = x_own[...]
-    distances = (2, 1, 3, 0)
-    owners = [(x + d) % N_X for d in distances]
-    for j, owner in enumerate(owners):
-        pair_out[j] = product(panel[2 * owner + 1 - core], value).astype(BF16)
-        send(always, pair_out.at[j], pair_in.at[j], 64 + j, pair_sem.at[j], sibling)
+    send(always, x_own, x_mate, 64, mate_sem.at[0], sibling)
+    load_ours.wait()
+    half_panel = panel[0].reshape(4 * 2 * half, 2 * half)
+    ours[...] = product(half_panel, x_own[...]).reshape(4, 2 * half, width)
+    arrived(panel.at[1], mate_sem.at[1])
+    arrived(x_mate, mate_sem.at[0])
 
     @pl.when(low_rows & (col < 2))
     def _():
         pl.semaphore_wait(go_sem, 1)
 
-    for j, (d, owner) in enumerate(zip(distances, owners)):
-        total = product(panel[2 * owner + core], value)
-        arrived(pair_in.at[j], pair_sem.at[j])
-        total = total + pair_in[j].astype(F32)
+    value = x_mate[...]
+    for j, d in enumerate((2, 1, 3, 0)):
+        owner = (x + d) % N_X
+        total = ours[owner] + product(panel[1, owner], value)
         if d > 0:
             sums[j] = total.astype(BF16)
             send(always, sums.at[j], cross_in.at[d - 1], 68 + j, cross_sem.at[d - 1], (row, owner * 2 + core))
@@ -592,16 +617,68 @@
         for buffer in buffers:
             if buffer.shape == shape and buffer.dtype == dtype:
                 return buffer
-        if shape == panel.shape[1:]:
-            return panel.at[0]
+        if shape == first.shape:
+            return first
         return part(0, 0, shape[1] // quarter - 1)
 
+    remote(panel.at[1], panel.at[1], 65, mate_sem.at[1], sibling).wait_send()
+
+    def sent(s, shape, dtype):
+        ref = same_size(shape, dtype)
+        remote(ref, ref, s, x_sem, sibling).wait_send()
+
+    groups = {}
     for when, s, shape, dtype in pending:
-
-        @pl.when(here(when) if isinstance(when, tuple) else when() if callable(when) else when)
-        def _(s=s, shape=shape, dtype=dtype):
-            ref = same_size(shape, dtype)
-            remote(ref, ref, s, x_sem, sibling).wait_send()
+        if isinstance(when, tuple):
+            groups.setdefault(when[0], {}).setdefault(when[1], []).append((s, shape, dtype))
+        elif when is always:
+            sent(s, shape, dtype)
+
+    def sent_in_row(r):
+        @pl.when(row == r)
+        def _():
+            for c, copies in groups[r].items():
+
+                @pl.when(col == c)
+                def _(copies=copies):
+                    for copy in copies:
+                        sent(*copy)
+
+    @pl.when(y == 0)
+    def _():
+        for r in groups:
+            if r < N_Z:
+                sent_in_row(r)
+        for when, s, shape, dtype in pending:
+            if not isinstance(when, tuple) and when is not always and when is not relay:
+
+                @pl.when(when)
+                def _(s=s, shape=shape, dtype=dtype):
+                    sent(s, shape, dtype)
+
+    @pl.when(y != 0)
+    def _():
+        for r in groups:
+            if r >= N_Z:
+                sent_in_row(r)
+
+        @pl.when(relay)
+        def _():
+            for when, s, shape, dtype in pending:
+                if when is relay:
+                    sent(s, shape, dtype)
+
+    @pl.when(is_relay)
+    def _():
+        for k, waits in relay_waits.items():
+
+            @pl.when((core == k % 2) & (z == (2 if k < 4 else 6)))
+            def _(waits=waits):
+                for wanted, s in waits:
+
+                    @pl.when(wanted())
+                    def _(s=s):
+                        remote(relays.at[0], relays.at[0], s, x_sem, sibling).wait_send()
 
 
 def body(lower, slab, inverses):
@@ -610,7 +687,8 @@
     vmem = pltpu.VMEM
     dma = pltpu.SemaphoreType.DMA
     scratch = [
-        vmem((row_blocks, order, order), BF16),
+        vmem((order, order), BF16),
+        vmem((2, row_blocks // 2, order, order), BF16),
         vmem((order, order), F32),
         vmem((4, 2, order, order), BF16),
         vmem((5, order, order), BF16),
@@ -625,8 +703,8 @@
         vmem((2, order, width), F32),
         vmem((2, order, width), BF16),
         vmem((2, order // 4, width), BF16),
-        vmem((4, order, width), BF16),
-        vmem((4, order, width), BF16),
+        vmem((order, width), BF16),
+        vmem((4, order, width), F32),
         vmem((3, order, width), BF16),
         vmem((3, order, width), BF16),
         dma((5,)),
@@ -640,7 +718,7 @@
         dma((5,)),
         dma((4,)),
         dma((4,)),
-        dma((4,)),
+        dma((2,)),
         dma((3,)),
     ]
     result = pl.pallas_call(
@@ -654,7 +732,7 @@
             collective_id=0, has_side_effects=True, vmem_limit_bytes=53 << 20
         ),
     )(
-        lower.reshape(row_blocks, order, order),
+        lower.reshape(row_blocks // 2, 2, order, order),
         slab.reshape(row_blocks, order, width),
         inverses.reshape(order, order),
     )

time: 55.6 us -> 55 us (0.989)
  Pallas kernels: 54.1 us -> 53.3 us
    pallas_call x1, Pallas kernels: 54.1 us -> 53.3 us  [body(): pl.pallas_call(kernel, name='window_solve', out_shape=jax.ShapeDtypeStruc...]
where the time goes in v5:
time: 55 us; the launch traced here: 54 us
  Pallas kernels  53.3 us (97%)
  local copies, waits for them, and re-layouts  0.71 us (1%)
    pallas_call x1, Pallas kernels, body(): pl.pallas_call(kernel, name='window_solve', out_shape=jax.ShapeDtypeStruc...  53.3 us

profile of v5, /device:TPU:21, one launch (start us, length us, event | category | flops | bytes accessed | tf_op | source)
XLA Modules:
  0.0 54.0 jit_solution(11632302327135237330)
XLA Ops:
  0.0 53.3 %window_solve.1 = f32[512,128]{1,0:T(8,128)S(1)} custom-call(bf16[4,2,512,512]{3,2,1,0:T(8,128)(2,1)} %bitcast.5, f32[8,512,128]{2,1,0:T(8,128)} %bitcast.6, f32[512,512]{1,0:T(8,128)} %bitcast.7), custom_call_target="tpu_custom_call" | custom-call | tf_op jit(solution)/shard_map/window_solve/pallas_call | solution.py:724
  53.3 0.7 %copy.5 = f32[1,1,512,128]{3,2,1,0:T(8,128)} copy(f32[1,1,512,128]{3,2,1,0:T(8,128)S(1)} %bitcast.4) | data formatting | bytes 524288

commit v6 on v5

--- a/solution.py
+++ b/solution.py
@@ -229,13 +229,9 @@
         low = (total - high.astype(F32)).astype(BF16)
         both = jnp.concatenate([high, low], axis=1)
 
-        def times(rows, depth):
-            done = jnp.dot(inv_parts[slot, 0, rows, :depth], both[:depth], preferred_element_type=F32)
-            if low_part:
-                done += jnp.dot(inv_parts[slot, 1, rows, :depth], both[:depth], preferred_element_type=F32)
-            return done
-
-        whole = jnp.concatenate([times(slice(0, half), half), times(slice(half, 2 * half), 2 * half)], axis=0)
+        whole = product(inv_parts[slot, 0], both)
+        if low_part:
+            whole += product(inv_parts[slot, 1], both)
         return whole[:, :width] + whole[:, width:]
 
     def product(block, value):
@@ -436,11 +432,10 @@
         for i, r in enumerate((4, 7)):
             send(when, x_stage.at[0], x_own, 20 + i, x_sem, (r, 2))
         scatter(when, 0, 2, 26)
-        arrived(blocks.at[0], block_sem.at[0])
+        for slot in range(2):
+            arrived(blocks.at[slot], block_sem.at[slot])
         arrived(acc_b.at[0], acc_b_sem.at[0])
-        stage_f[0] = acc_b[0].astype(F32) - product(blocks[0], x_own[...])
-        arrived(blocks.at[1], block_sem.at[1])
-        total = stage_f[0] - product(blocks[1], x_stage[0])
+        total = acc_b[0].astype(F32) - (product(blocks[0], x_own[...]) + product(blocks[1], x_stage[0]))
         inverse_arrived(1)
         value = solve(1, total)
         x_stage[1] = value.astype(BF16)
@@ -481,11 +476,7 @@
                         pl.semaphore_signal(go_sem, inc=1, device_id=(r, c), device_id_type=MESH)
                 block = first[...] if target == r else blocks[0]
                 stage_b[i] = (stage_f[j] - product(block, x_own[...])).astype(BF16)
-                if target == 6:
-                    pl.semaphore_wait(go_sem, 1)
                 send((r, 3), stage_b.at[i], acc_b.at[target - 4], 18 + i, acc_b_sem.at[target - 4], SOLVE_47)
-                if target == 5:
-                    pl.semaphore_signal(go_sem, inc=1, device_id=(7, 3), device_id_type=MESH)
 
     @pl.when(here(SOLVE_47))
     def _():
@@ -501,21 +492,19 @@
         for slot in range(1, 4):
             inverse_arrived(slot)
         for q in range(4):
-            for j in range(q - 1):
-                done = product(place[q, j][...], x_stage[j])
-                acc_f[q] = done if j == 0 else acc_f[q] + done
             arrived(acc_b.at[q], acc_b_sem.at[q])
             total = acc_b[q].astype(F32)
-            if q > 1:
+            if q > 0:
                 total -= acc_f[q]
-            if q > 0:
-                total -= product(place[q, q - 1][...], x_stage[q - 1])
             value = solve(q, total)
             x_stage[q] = value.astype(BF16)
             x_full[q] = value
             scatter(when, q, 4 + q, 20 + 4 * q)
             if q < 2:
                 send(when, x_full.at[q], x_in, 36 + q, x_in_sem, (4 + q, 0))
+            for r in range(q + 1, 4):
+                done = product(place[r, q][...], x_stage[q])
+                acc_f[r] = done if q == 0 else acc_f[r] + done
         send(when, x_full.at[2], x_in, 38, x_in_sem, (6, 0))
     for k in range(2, 8):
         relay_quarter(k)

time: 55 us -> 54.5 us (level)
  no operation moved by 1% of the time
where the time goes in v6:
time: 54.5 us; the launch traced here: 53.7 us
  Pallas kernels  52.9 us (97%)
  local copies, waits for them, and re-layouts  0.71 us (1%)
    pallas_call x1, Pallas kernels, body(): pl.pallas_call(kernel, name='window_solve', out_shape=jax.ShapeDtypeStruc...  52.9 us

profile of v6, /device:TPU:21, one launch (start us, length us, event | category | flops | bytes accessed | tf_op | source)
XLA Modules:
  0.0 53.7 jit_solution(11820505659223086214)
XLA Ops:
  0.0 52.9 %window_solve.1 = f32[512,128]{1,0:T(8,128)S(1)} custom-call(bf16[4,2,512,512]{3,2,1,0:T(8,128)(2,1)} %bitcast.5, f32[8,512,128]{2,1,0:T(8,128)} %bitcast.6, f32[512,512]{1,0:T(8,128)} %bitcast.7), custom_call_target="tpu_custom_call" | custom-call | tf_op jit(solution)/shard_map/window_solve/pallas_call | solution.py:713
  52.9 0.7 %copy.5 = f32[1,1,512,128]{3,2,1,0:T(8,128)} copy(f32[1,1,512,128]{3,2,1,0:T(8,128)S(1)} %bitcast.4) | data formatting | bytes 524288

commit v7 on v6

--- a/solution.py
+++ b/solution.py
@@ -123,63 +123,7 @@
     def greet(device):
         pl.semaphore_signal(barrier, inc=1, device_id=device, device_id_type=MESH)
 
-    greet(sibling)
-    for d in range(1, N_X):
-        greet((row, (x + d) % N_X * 2 + core))
-    count = jnp.int32(N_X)
-    is_root = (z == root_z) & (col < 2)
-    in_other = (col < 2) & (y != 0)
-
-    @pl.when(is_root & in_other)
-    def _():
-        for d in range(1, N_Z):
-            greet((y * N_Z + (z + d) % N_Z, col))
-
-    @pl.when(jnp.logical_not(is_root) & in_other)
-    def _():
-        greet((y * N_Z + root_z, col))
-
-    count += jnp.where(in_other, jnp.where(is_root, N_Z - 1, 1), 0)
-    is_relay = (z == 2) | (z == 6)
-    relay_z = jnp.where(col < 4, 2, 6)
-
-    @pl.when(is_relay)
-    def _():
-        for k in range(2, 8):
-
-            @pl.when((core == k % 2) & (z == (2 if k < 4 else 6)))
-            def _(k=k):
-                for d in range(1, N_Z):
-                    greet((y * N_Z + (z + d) % N_Z, k))
-
-                @pl.when(col != k)
-                def _():
-                    greet((row, k))
-
-    count += jnp.where(z == 2, N_Z - 1 + jnp.where(x == 1, 0, 1), 0)
-    count += jnp.where(z == 6, 2 * (N_Z - 1) + jnp.where(x >= 2, 1, 2), 0)
-
-    @pl.when(col >= 2)
-    def _():
-        for q in range(N_X):
-
-            @pl.when((z != relay_z) | (q != x))
-            def _(q=q):
-                greet((y * N_Z + relay_z, 2 * q + core))
-
-    count += jnp.where(col >= 2, jnp.where(z == jnp.where(col < 4, 2, 6), N_X - 1, N_X), 0)
-    in_line = is_root | is_relay
-
-    @pl.when(in_line & (y == 0))
-    def _():
-        for d in range(1, N_Y):
-            greet((d * N_Z + z, col))
-
-    @pl.when(in_line & (y != 0))
-    def _():
-        greet((z, col))
-
-    count += jnp.where(in_line, jnp.where(y == 0, N_Y - 1, 1), 0)
+    count = jnp.int32(0)
     partners = {}
     for a, b in special_pairs():
         partners.setdefault(a, []).append(b)
@@ -211,6 +155,63 @@
             if r >= N_Z:
                 greet_row(r)
 
+    greet(sibling)
+    for d in range(1, N_X):
+        greet((row, (x + d) % N_X * 2 + core))
+    count += N_X
+    is_root = (z == root_z) & (col < 2)
+    in_other = (col < 2) & (y != 0)
+
+    @pl.when(is_root & in_other)
+    def _():
+        for d in range(1, N_Z):
+            greet((y * N_Z + (z + d) % N_Z, col))
+
+    @pl.when(jnp.logical_not(is_root) & in_other)
+    def _():
+        greet((y * N_Z + root_z, col))
+
+    count += jnp.where(in_other, jnp.where(is_root, N_Z - 1, 1), 0)
+    is_relay = (z == 2) | (z == 6)
+    relay_z = jnp.where(col < 4, 2, 6)
+
+    @pl.when(is_relay)
+    def _():
+        for k in range(2, 8):
+
+            @pl.when((core == k % 2) & (z == (2 if k < 4 else 6)))
+            def _(k=k):
+                for d in range(1, N_Z):
+                    greet((y * N_Z + (z + d) % N_Z, k))
+
+                @pl.when(col != k)
+                def _():
+                    greet((row, k))
+
+    count += jnp.where(z == 2, N_Z - 1 + jnp.where(x == 1, 0, 1), 0)
+    count += jnp.where(z == 6, 2 * (N_Z - 1) + jnp.where(x >= 2, 1, 2), 0)
+
+    @pl.when(col >= 2)
+    def _():
+        for q in range(N_X):
+
+            @pl.when((z != relay_z) | (q != x))
+            def _(q=q):
+                greet((y * N_Z + relay_z, 2 * q + core))
+
+    count += jnp.where(col >= 2, jnp.where(z == jnp.where(col < 4, 2, 6), N_X - 1, N_X), 0)
+    in_line = is_root | is_relay
+
+    @pl.when(in_line & (y == 0))
+    def _():
+        for d in range(1, N_Y):
+            greet((d * N_Z + z, col))
+
+    @pl.when(in_line & (y != 0))
+    def _():
+        greet((z, col))
+
+    count += jnp.where(in_line, jnp.where(y == 0, N_Y - 1, 1), 0)
     def split_inverse(slot):
         value = inv[...]
         high = value.astype(BF16)
@@ -286,11 +287,11 @@
             send(when, x_own, x_own, 9 + i, x_sem, (target, c))
         if c == 0:
             send(when, x_own, x_stage.at[0], 19, side_sem, (0, 1))
-        for d in (2, 1, 3):
-            send(when, x_own, x_own, 15 + d, x_sem, (d * N_Z + root_row, c))
         for i, target in enumerate(in_plane[c]):
             if i > 0:
                 send(when, x_own, x_own, 9 + i, x_sem, (target, c))
+        for d in (2, 1, 3):
+            send(when, x_own, x_own, 15 + d, x_sem, (d * N_Z + root_row, c))
 
     @pl.when(here(SOLVE_0))
     def _():

time: 54.5 us -> 54.5 us (level)
  no operation moved by 1% of the time
where the time goes in v7:
time: 54.5 us; the launch traced here: 53.6 us
  Pallas kernels  52.9 us (97%)
  local copies, waits for them, and re-layouts  0.71 us (1%)
    pallas_call x1, Pallas kernels, body(): pl.pallas_call(kernel, name='window_solve', out_shape=jax.ShapeDtypeStruc...  52.9 us

profile of v7, /device:TPU:21, one launch (start us, length us, event | category | flops | bytes accessed | tf_op | source)
XLA Modules:
  0.0 53.6 jit_solution(5836510341734306214)
XLA Ops:
  0.0 52.9 %window_solve.1 = f32[512,128]{1,0:T(8,128)S(1)} custom-call(bf16[4,2,512,512]{3,2,1,0:T(8,128)(2,1)} %bitcast.5, f32[8,512,128]{2,1,0:T(8,128)} %bitcast.6, f32[512,512]{1,0:T(8,128)} %bitcast.7), custom_call_target="tpu_custom_call" | custom-call | tf_op jit(solution)/shard_map/window_solve/pallas_call | solution.py:714
  52.9 0.7 %copy.5 = f32[1,1,512,128]{3,2,1,0:T(8,128)} copy(f32[1,1,512,128]{3,2,1,0:T(8,128)S(1)} %bitcast.4) | data formatting | bytes 524288

commit v8 on v7

--- a/solution.py
+++ b/solution.py
@@ -57,7 +57,7 @@
     lower, slab, inverses, out,
     first, panel, inv, inv_parts, blocks, right, right_own, x_own, x_stage, x_full, x_in,
     acc_f, acc_b, stage_f, stage_b, relays, x_mate, ours, sums, cross_in,
-    load_sem, send_sem, x_sem, x_in_sem, side_sem, go_sem, relay_sem, inv_sem, block_sem, acc_f_sem, acc_b_sem, mate_sem, cross_sem,
+    load_sem, send_sem, x_sem, x_in_sem, side_sem, relay_sem, inv_sem, block_sem, acc_f_sem, acc_b_sem, mate_sem, cross_sem,
 ):
     row = lax.axis_index("row")
     col = lax.axis_index("col")
@@ -473,8 +473,6 @@
                 stage_f[j] = acc_b[j].astype(F32) - acc_f[j]
                 if i == 0:
                     arrived(x_own, x_sem)
-                    for c in (0, 1):
-                        pl.semaphore_signal(go_sem, inc=1, device_id=(r, c), device_id_type=MESH)
                 block = first[...] if target == r else blocks[0]
                 stage_b[i] = (stage_f[j] - product(block, x_own[...])).astype(BF16)
                 send((r, 3), stage_b.at[i], acc_b.at[target - 4], 18 + i, acc_b_sem.at[target - 4], SOLVE_47)
@@ -552,10 +550,6 @@
     ours[...] = product(half_panel, x_own[...]).reshape(4, 2 * half, width)
     arrived(panel.at[1], mate_sem.at[1])
     arrived(x_mate, mate_sem.at[0])
-
-    @pl.when(low_rows & (col < 2))
-    def _():
-        pl.semaphore_wait(go_sem, 1)
 
     value = x_mate[...]
     for j, d in enumerate((2, 1, 3, 0)):
@@ -702,7 +696,6 @@
         dma,
         dma,
         dma,
-        pltpu.SemaphoreType.REGULAR,
         dma((2,)),
         dma((4, 2, 4)),
         dma((5,)),

time: 54.5 us -> 54.5 us (level)
  no operation moved by 1% of the time
where the time goes in v8:
time: 54.5 us; the launch traced here: 53.7 us
  Pallas kernels  53 us (97%)
  local copies, waits for them, and re-layouts  0.71 us (1%)
    pallas_call x1, Pallas kernels, body(): pl.pallas_call(kernel, name='window_solve', out_shape=jax.ShapeDtypeStruc...  53 us

profile of v8, /device:TPU:21, one launch (start us, length us, event | category | flops | bytes accessed | tf_op | source)
XLA Modules:
  0.0 53.7 jit_solution(11792808308682338097)
XLA Ops:
  0.0 53.0 %window_solve.1 = f32[512,128]{1,0:T(8,128)S(1)} custom-call(bf16[4,2,512,512]{3,2,1,0:T(8,128)(2,1)} %bitcast.5, f32[8,512,128]{2,1,0:T(8,128)} %bitcast.6, f32[512,512]{1,0:T(8,128)} %bitcast.7), custom_call_target="tpu_custom_call" | custom-call | tf_op jit(solution)/shard_map/window_solve/pallas_call | solution.py:707
  53.0 0.7 %copy.5 = f32[1,1,512,128]{3,2,1,0:T(8,128)} copy(f32[1,1,512,128]{3,2,1,0:T(8,128)S(1)} %bitcast.4) | data formatting | bytes 524288
